TPU v7x, 32 devices: a whole 2x2x4 slice. The times are simulated.
32 devices in a mesh: dp: 8 (over z, x), heads: 4 (over y, core).
Axes of the slice: x: 2, y: 2, z: 4, core: 2. Of those that a mesh axis runs over, the one named last changes fastest.
Arguments:
- tokens: bfloat16 [24576, 480], P(('dp', 'heads')), may hold values from -6 to 6
- attn_norm_gain: float32 [480], replicated, may hold values from 0.5 to 1.5
- attn_norm_bias: float32 [480], replicated, may hold values from -3 to 3
- qkv_weight: bfloat16 [480, 1440], P(None, 'heads'), may hold values from -0.25 to 0.25
- qkv_bias: float32 [1440], P('heads'), may hold values from -3 to 3
- out_weight: bfloat16 [480, 480], P('heads'), may hold values from -0.75 to 0.75
- out_bias: float32 [480], replicated, may hold values from -2 to 2
- ffn_norm_gain: float32 [480], replicated, may hold values from 0.5 to 1.5
- ffn_norm_bias: float32 [480], replicated, may hold values from -3 to 3
- up_weight: bfloat16 [480, 1920], P('heads', 'dp'), may hold values from -0.25 to 0.25
- up_bias: float32 [1920], replicated, may hold values from -3 to 3
- down_weight: bfloat16 [1920, 480], P('dp', 'heads'), may hold values from -0.125 to 0.125
- down_bias: float32 [480], replicated, may hold values from -2 to 2
- lengths: int32 [24, 4], P('dp'), may hold values from 0 to 1024, as said below
- cluster_ids: int32 [24, 4], P('dp'), may hold values from 0 to 1023
- cluster_weight: float32 [1024], replicated, may hold values from 0.25 to 4
- grad_out: bfloat16 [24576, 480], P(('dp', 'heads')), may hold values from -6 to 6
Outputs:
- result: bfloat16 [24576, 480], P(('dp', 'heads'))
- d_tokens: float32 [24576, 480], P(('dp', 'heads'))
- d_attn_norm_gain: float32 [480], replicated
- d_attn_norm_bias: float32 [480], replicated
- d_qkv_weight: float32 [480, 1440], P(None, 'heads')
- d_qkv_bias: float32 [1440], P('heads')
- d_out_weight: float32 [480, 480], P('heads')
- d_out_bias: float32 [480], replicated
- d_ffn_norm_gain: float32 [480], replicated
- d_ffn_norm_bias: float32 [480], replicated
- d_up_weight: float32 [480, 1920], P('heads', 'dp')
- d_up_bias: float32 [1920], replicated
- d_down_weight: float32 [1920, 480], P('dp', 'heads')
- d_down_bias: float32 [480], replicated
Inputs may be any that keep to these rules, and one draw needn't show every extreme that they name: `lengths`: in each group the 4 slots are proteins lying one after another from the group's first row, summing to at most 1024, the remaining rows padding. The third slot's protein starts before row 256 of its group and ends after row 768; in some group it is 1024 long.
All inputs are finite; a program needn't handle non-finite values.
Results may differ from a plain program's by a relative error of at most 0.015.
Values may be sent and summed in bfloat16 or wider, within the bound.
A program may use at most 256 MiB of HBM per device.

v0:
```python
from functools import partial

import jax
import jax.numpy as jnp
from jax import lax
from jax.sharding import PartitionSpec as P

HD = 24


EPSILON = 1e-05


def layer_norm(values, scale_vec, shift_vec):
    average = jnp.mean(values, axis=-1, keepdims=True)
    centred = values - average
    variance = jnp.mean(centred * centred, axis=-1, keepdims=True)
    return centred * lax.rsqrt(variance + EPSILON) * scale_vec + shift_vec


def rotate(vectors, cos_table, sin_table):
    half_size = vectors.shape[-1] // 2
    first_half = vectors[..., :half_size]
    second_half = vectors[..., half_size:]
    return jnp.concatenate(
        [
            first_half * cos_table - second_half * sin_table,
            second_half * cos_table + first_half * sin_table,
        ],
        axis=-1,
    )


def angles(position, head_size):
    frequency = 10000.0 ** (-2.0 * jnp.arange(head_size // 2, dtype=jnp.float32) / head_size)
    turn_angle = position[:, None] * frequency[None, :]
    return (jnp.cos(turn_angle)[:, None, :], jnp.sin(turn_angle)[:, None, :])


def structure(lengths_row, ids_row, weight_table, row_total):
    protein_ends = jnp.cumsum(lengths_row, dtype=jnp.int32)
    row_index = jnp.arange(row_total, dtype=jnp.int32)
    passed_ends = (row_index[:, None] >= protein_ends[None, :]).astype(jnp.int32)
    segment = jnp.sum(passed_ends, axis=1, dtype=jnp.int32)
    offset = jnp.sum(passed_ends * lengths_row[None, :], axis=1, dtype=jnp.int32)
    position = (row_index - offset).astype(jnp.float32)
    slot_ids = jnp.arange(lengths_row.shape[0], dtype=jnp.int32)
    member = (segment[:, None] == slot_ids[None, :]).astype(jnp.float32)
    row_weight = jnp.sum(member * weight_table[ids_row][None, :], axis=1)
    return (segment, position, row_weight)


def contract_rows(left_side, right_side):
    return lax.dot_general(
        left_side, right_side, (((0,), (0,)), ((), ())), preferred_element_type=jnp.float32
    )


def contract_cols(left_side, right_side):
    return lax.dot_general(
        left_side, right_side, (((1,), (1,)), ((), ())), preferred_element_type=jnp.float32
    )


def masked_scores(query_block, key_rows, segment_block, segment):
    scores = jnp.einsum("qhd,khd->hqk", query_block, key_rows, preferred_element_type=jnp.float32)
    allowed = segment_block[:, None] == segment[None, :]
    return jnp.where(allowed[None], scores, -1e30)


def device_order(rows, group_count, heads_count):
    width = rows.shape[-1]
    return (
        rows.reshape(group_count, heads_count, rows.shape[0] // (group_count * heads_count), width)
        .transpose(1, 0, 2, 3)
        .reshape(rows.shape[0], width)
    )


def local(
    tokens,
    attn_norm_gain,
    attn_norm_bias,
    qkv_weight,
    qkv_bias,
    out_weight,
    out_bias,
    ffn_norm_gain,
    ffn_norm_bias,
    up_weight,
    up_bias,
    down_weight,
    down_bias,
    lengths,
    cluster_ids,
    cluster_weight,
    grad_out,
):
    own_rows = tokens.shape[0]
    heads_count = lax.axis_size("heads")
    group_count = lengths.shape[0]
    group_dev = own_rows // group_count
    group_rows = group_dev * heads_count
    all_rows = group_count * group_rows
    model_width = tokens.shape[1]
    local_heads = out_weight.shape[0] // HD
    first_row = lax.axis_index("heads") * group_dev
    segment, position, row_weight = jax.vmap(
        lambda lengths_row, ids_row: structure(lengths_row, ids_row, cluster_weight, group_rows)
    )(lengths, cluster_ids)
    own_weight = lax.dynamic_slice_in_dim(row_weight, first_row, group_dev, 1).reshape(own_rows)
    tokens_full = tokens.astype(jnp.float32)
    normed_one, pull_one = jax.vjp(layer_norm, tokens_full, attn_norm_gain, attn_norm_bias)
    normed_low = normed_one.astype(jnp.bfloat16).reshape(group_count, group_dev, model_width)
    qkv_proj = (
        jnp.einsum(
            "grd,dc->grc",
            lax.all_gather(normed_low, "heads", axis=1, tiled=True),
            qkv_weight,
            preferred_element_type=jnp.float32,
        )
        + qkv_bias
    )
    qkv_proj = qkv_proj.reshape(all_rows, local_heads, 3, HD)
    cos_table, sin_table = angles(position.reshape(all_rows), HD)

    def turn_pair(pair_rows):
        return jnp.stack(
            [
                rotate(pair_rows[:, :, 0], cos_table, sin_table) * HD ** (-0.5),
                rotate(pair_rows[:, :, 1], cos_table, sin_table),
            ],
            axis=2,
        )

    turned, pull_turn = jax.vjp(turn_pair, qkv_proj[:, :, :2])
    queries = turned[:, :, 0].astype(jnp.bfloat16)
    key_rows = turned[:, :, 1].astype(jnp.bfloat16)
    values = qkv_proj[:, :, 2].astype(jnp.bfloat16)
    block_rows = min(512, group_rows)
    block_count = group_rows // block_rows
    context_parts = []
    lse_parts = []
    for group_index in range(group_count):
        base = group_index * group_rows
        group_keys = key_rows[base : base + group_rows]
        group_values = values[base : base + group_rows]
        group_segment = segment[group_index]
        for block_index in range(block_count):
            row_start = block_index * block_rows
            query_block = queries[base + row_start : base + row_start + block_rows]
            scores = masked_scores(
                query_block,
                group_keys,
                group_segment[row_start : row_start + block_rows],
                group_segment,
            )
            highest = jnp.max(scores, axis=-1, keepdims=True)
            exp_terms = jnp.exp(scores - highest)
            denominator = jnp.sum(exp_terms, axis=-1, keepdims=True)
            weights_low = (exp_terms / denominator).astype(jnp.bfloat16)
            context_parts.append(
                jnp.einsum(
                    "hqk,khd->qhd", weights_low, group_values, preferred_element_type=jnp.float32
                )
            )
            lse_parts.append(highest + jnp.log(denominator))
    context_low = (
        jnp.concatenate(context_parts, axis=0)
        .reshape(all_rows, local_heads * HD)
        .astype(jnp.bfloat16)
    )
    context_dev = device_order(context_low, group_count, heads_count)
    shard_rows = context_dev
    attn_own = (
        lax.psum_scatter(
            jnp.dot(shard_rows, out_weight, preferred_element_type=jnp.float32),
            "heads",
            scatter_dimension=0,
            tiled=True,
        )
        + out_bias
    )
    middle = tokens_full + attn_own
    normed_two, pull_two = jax.vjp(layer_norm, middle, ffn_norm_gain, ffn_norm_bias)
    normed_two_low = normed_two.astype(jnp.bfloat16)
    up_part, down_part = (
        lax.all_gather(up_weight, "dp", axis=1, tiled=True),
        lax.all_gather(down_weight, "dp", axis=0, tiled=True),
    )
    up_full, down_full = (
        lax.all_gather(up_part, "heads", axis=0, tiled=True),
        lax.all_gather(down_part, "heads", axis=1, tiled=True),
    )
    up_proj = jnp.dot(normed_two_low, up_full, preferred_element_type=jnp.float32) + up_bias
    hidden, pull_gelu = jax.vjp(partial(jax.nn.gelu, approximate=False), up_proj)
    hidden_low = hidden.astype(jnp.bfloat16)
    ffn_out = jnp.dot(hidden_low, down_full, preferred_element_type=jnp.float32) + down_bias
    result = (middle + ffn_out).astype(jnp.bfloat16)
    d_result = grad_out.astype(jnp.float32) * own_weight[:, None]
    d_ffn = d_result.astype(jnp.bfloat16)
    d_down_bias = jnp.sum(d_ffn.astype(jnp.float32), axis=0)
    d_down = contract_rows(hidden_low, d_ffn)
    d_hidden = contract_cols(d_ffn, down_full)
    (d_up_proj,) = pull_gelu(d_hidden)
    d_up_low = d_up_proj.astype(jnp.bfloat16)
    d_up_bias = jnp.sum(d_up_low.astype(jnp.float32), axis=0)
    d_up = contract_rows(normed_two_low, d_up_low)
    d_normed_two = contract_cols(d_up_low, up_full)
    d_middle_norm, d_ffn_gain, d_ffn_shift = pull_two(d_normed_two)
    d_middle = d_result + d_middle_norm
    d_attn = d_middle.astype(jnp.bfloat16)
    d_out_bias = jnp.sum(d_attn.astype(jnp.float32), axis=0)
    context_group = context_low.reshape(group_count, group_rows, local_heads * HD)
    d_attn_groups = d_attn.reshape(group_count, group_dev, model_width)
    shard_rows = lax.all_gather(d_attn_groups, "heads", axis=1, tiled=True)
    part_grad = jnp.einsum(
        "grd,cd->grc", shard_rows, out_weight, preferred_element_type=jnp.float32
    )
    d_out_acc = jnp.einsum(
        "grc,grd->cd", context_group, shard_rows, preferred_element_type=jnp.float32
    )
    d_out_weight = d_out_acc
    d_context_low = part_grad.astype(jnp.bfloat16).reshape(all_rows, local_heads, HD)
    d_query_parts = []
    d_key_parts = []
    d_value_parts = []
    for group_index in range(group_count):
        base = group_index * group_rows
        group_keys = key_rows[base : base + group_rows]
        group_values = values[base : base + group_rows]
        group_segment = segment[group_index]
        d_keys = jnp.zeros((group_rows, local_heads, HD), jnp.float32)
        d_values = jnp.zeros((group_rows, local_heads, HD), jnp.float32)
        for block_index in range(block_count):
            row_start = block_index * block_rows
            query_block = queries[base + row_start : base + row_start + block_rows]
            scores = masked_scores(
                query_block,
                group_keys,
                group_segment[row_start : row_start + block_rows],
                group_segment,
            )
            prob_full = jnp.exp(scores - lse_parts[group_index * block_count + block_index])
            weights_low = prob_full.astype(jnp.bfloat16)
            grad_block = d_context_low[base + row_start : base + row_start + block_rows]
            d_prob = jnp.einsum(
                "qhd,khd->hqk", grad_block, group_values, preferred_element_type=jnp.float32
            )
            row_inner = jnp.sum(prob_full * d_prob, axis=-1, keepdims=True)
            d_scores = (prob_full * (d_prob - row_inner)).astype(jnp.bfloat16)
            d_query_parts.append(
                jnp.einsum("hqk,khd->qhd", d_scores, group_keys, preferred_element_type=jnp.float32)
            )
            d_keys = d_keys + jnp.einsum(
                "hqk,qhd->khd", d_scores, query_block, preferred_element_type=jnp.float32
            )
            d_values = d_values + jnp.einsum(
                "hqk,qhd->khd", weights_low, grad_block, preferred_element_type=jnp.float32
            )
        d_key_parts.append(d_keys)
        d_value_parts.append(d_values)
    d_turned = jnp.stack(
        [jnp.concatenate(d_query_parts, axis=0), jnp.concatenate(d_key_parts, axis=0)], axis=2
    )
    (d_pair,) = pull_turn(d_turned)
    d_values_all = jnp.concatenate(d_value_parts, axis=0)
    d_qkv = (
        jnp.concatenate([d_pair, d_values_all[:, :, None]], axis=2)
        .reshape(all_rows, local_heads * 3 * HD)
        .astype(jnp.bfloat16)
    )
    d_qkv_bias = jnp.sum(d_qkv.astype(jnp.float32), axis=0)
    d_qkv_group = d_qkv.reshape(group_count, group_rows, local_heads * 3 * HD)
    grad_rows = d_qkv_group
    d_qkv_weight = jnp.einsum(
        "grd,grc->dc",
        lax.all_gather(normed_low, "heads", axis=1, tiled=True),
        grad_rows,
        preferred_element_type=jnp.float32,
    )
    d_qkv_dev = device_order(d_qkv, group_count, heads_count)
    grad_rows = d_qkv_dev
    d_normed_one = lax.psum_scatter(
        contract_cols(grad_rows, qkv_weight).astype(jnp.bfloat16),
        "heads",
        scatter_dimension=0,
        tiled=True,
    ).astype(jnp.float32)
    d_tokens_norm, d_attn_gain, d_attn_shift = pull_one(d_normed_one)
    d_tokens = d_middle + d_tokens_norm
    d_qkv_weight, d_qkv_bias, d_out_weight = lax.psum(
        (d_qkv_weight, d_qkv_bias, d_out_weight), "dp"
    )
    d_attn_gain, d_attn_shift, d_out_bias, d_ffn_gain, d_ffn_shift, d_up_bias, d_down_bias = (
        lax.psum(
            (
                d_attn_gain,
                d_attn_shift,
                d_out_bias,
                d_ffn_gain,
                d_ffn_shift,
                d_up_bias,
                d_down_bias,
            ),
            ("dp", "heads"),
        )
    )
    up_section, down_section = (
        lax.psum_scatter(
            d_up.astype(jnp.bfloat16), "heads", scatter_dimension=0, tiled=True
        ).astype(jnp.float32),
        lax.psum_scatter(
            d_down.astype(jnp.bfloat16), "heads", scatter_dimension=1, tiled=True
        ).astype(jnp.float32),
    )
    d_up_weight, d_down_weight = (
        lax.psum_scatter(up_section, "dp", scatter_dimension=1, tiled=True),
        lax.psum_scatter(down_section, "dp", scatter_dimension=0, tiled=True),
    )
    return (
        result,
        d_tokens,
        d_attn_gain,
        d_attn_shift,
        d_qkv_weight,
        d_qkv_bias,
        d_out_weight,
        d_out_bias,
        d_ffn_gain,
        d_ffn_shift,
        d_up_weight,
        d_up_bias,
        d_down_weight,
        d_down_bias,
    )


def solution(mesh):
    placed = (
        P(("dp", "heads"), None),
        P(),
        P(),
        P(None, "heads"),
        P("heads"),
        P("heads", None),
        P(),
        P(),
        P(),
        P("heads", "dp"),
        P(),
        P("dp", "heads"),
        P(),
        P("dp", None),
        P("dp", None),
        P(),
        P(("dp", "heads"), None),
    )
    return jax.shard_map(
        local,
        mesh=mesh,
        in_specs=placed,
        out_specs=(
            P(("dp", "heads"), None),
            P(("dp", "heads"), None),
            P(),
            P(),
            P(None, "heads"),
            P("heads"),
            P("heads", None),
            P(),
            P(),
            P(),
            P("heads", "dp"),
            P(),
            P("dp", "heads"),
            P(),
        ),
        check_vma=False,
    )
```

profile of v0, /device:TPU:0, one launch (start us, length us, event | category | flops | bytes accessed | tf_op | source)
XLA Modules:
  0.0 717.4 jit_solution(521506998257198735)
XLA Ops:
  18.0 26.6 %all-gather.5.cloned.1.call-done = bf16[3,1024,480]{1,2,0:T(8,128)(2,1)} async-done(((bf16[3,256,480]{1,2,0:T(8,128)(2,1)}), bf16[3,1024,480]{1,2,0:T(8,128)(2,1)}) %all-gather.5.cloned.1.call-update) | async-done | bytes 2949136 | tf_op jit(solution)/shard_map/all_gather | solution.py:118
  53.6 8.3 %reshape.465 = f32[3072,5,3,24]{0,3,2,1:T(8,128)} reshape(f32[3,1024,360]{1,0,2:T(4,128)} %copy.115) | data formatting | bytes 8847360 | tf_op jit(solution)/shard_map/reshape | solution.py:124
  98.0 6.7 fusion.5
  104.8 6.6 fusion.4
  111.3 6.6 fusion.1
  117.9 6.6 fusion
  130.6 6.2 fusion.90
  139.4 6.6 fusion.2
  155.4 6.2 fusion.84
  172.9 31.5 %all_gather.20 = bf16[120,1920]{0,1:T(8,128)(2,1)S(1)} all-gather(bf16[120,240]{0,1:T(8,128)(2,1)S(1)} %copy.120), channel_id=1, replica_groups=mesh['dp'=8,'heads'=4] {'dp'}, dimensions={1}, use_global_device_ids=true | all-gather | bytes 518400 | tf_op jit(solution)/shard_map/all_gather | solution.py:188
  205.4 31.2 %all_gather.22 = bf16[1920,120]{1,0:T(8,128)(2,1)S(1)} all-gather(bf16[240,120]{1,0:T(8,128)(2,1)S(1)} %copy-done.70), channel_id=1, replica_groups=mesh['dp'=8,'heads'=4] {'dp'}, dimensions={0}, use_global_device_ids=true | all-gather | bytes 518400 | tf_op jit(solution)/shard_map/all_gather | solution.py:189
  241.7 9.5 %all-gather.7.cloned.1.call-done = bf16[480,1920]{1,0:T(8,128)(2,1)} async-done(((bf16[120,1920]{1,0:T(8,128)(2,1)}), bf16[480,1920]{1,0:T(8,128)(2,1)}) %all-gather.7.cloned.1.call-update) | async-done | bytes 1843216 | tf_op jit(solution)/shard_map/all_gather | solution.py:192
  251.3 18.7 %multiply_convert_fusion.6 = (bf16[768,1920]{1,0:T(8,128)(2,1)}, f32[768,1920]{1,0:T(8,128)}, f32[768,1920]{1,0:T(8,128)}) fusion(f32[1920]{0:T(1024)S(1)} %copy-done.88, bf16[480,1920]{1,0:T(8,128)(2,1)} %all-gather.7.cloned.1.call-done, f32[768,480]{0,1:T(8,128)} %copy-done.19, f32[480]{0:T(512)S(1)} %copy-done.89, f32[480]{0:T(512)S(1)} %copy-done.84, ...), kind=kOutput, calls=%fused_computation.53 | convolution fusion | flops 1514741760 | bytes 18081024 | tf_op jit(solution)/shard_map/dot_general | solution.py:195
  274.0 8.2 %convert_reduce_fusion = (f32[1920]{0:T(1024)}, bf16[768,1920]{1,0:T(8,128)(2,1)S(1)}) fusion(f32[768,1920]{1,0:T(8,128)} %get-tuple-element.123, bf16[1920,480]{0,1:T(8,128)(2,1)} %all-gather.9.cloned.1.call-done, bf16[768,480]{0,1:T(8,128)(2,1)S(1)} %copy-done.34, f32[768]{0:T(1024)S(1)} %mul.361, f32[768,1920]{1,0:T(8,128)} %get-tuple-element.173, ...), kind=kOutput, calls=%fused_computation.51 | convolution fusion | flops 1441749120 | bytes 17344512 | tf_op jit(solution)/shard_map/dot_general | solution.py:60
  303.7 13.2 %reduce-scatter.23.cloned.1.call-done = bf16[120,1920]{1,0:T(8,128)(2,1)} async-done(((bf16[480,1920]{1,0:T(8,128)(2,1)}), bf16[120,1920]{1,0:T(8,128)(2,1)}) %reduce-scatter.23.cloned.1.call-update) | async-done | bytes 460816
  319.2 27.6 %all-gather.11.cloned.1.call-done = bf16[3,1024,480]{1,2,0:T(8,128)(2,1)} async-done(((bf16[3,256,480]{1,2,0:T(8,128)(2,1)}), bf16[3,1024,480]{1,2,0:T(8,128)(2,1)}) %all-gather.11.cloned.1.call-update) | async-done | bytes 2949136 | tf_op jit(solution)/shard_map/all_gather | solution.py:216
  353.5 7.1 fusion.18
  360.6 8.4 %multiply_reduce_fusion = (f32[5,512]{1,0:T(8,128)S(1)}, f32[5,512,1024]{2,1,0:T(8,128)}) fusion(f32[5,512,1024]{2,1,0:T(8,128)} %get-tuple-element.172, f32[5,512]{1,0:T(8,128)S(1)} %log_add_fusion, pred[512,1024]{1,0:T(8,128)(4,1)S(1)} %get-tuple-element.155, bf16[3072,5,3,24]{0,3,1,2:T(8,128)(2,1)} %copy-done.26, bf16[3072,5,24]{0,2,1:T(8,128)(2,1)S(1)} %reshape.468), kind=kOutput, calls=%fused_computation.2 | convolution fusion | flops 136312320 | bytes 21891072 | tf_op jit(solution)/shard_map/qhd,khd->hqk/dot_general | solution.py:247
  372.3 7.0 multiply_reduce_fusion.2
  379.3 6.4 fusion.26
  385.7 11.3 %multiply_reduce_fusion.4 = (f32[5,512]{1,0:T(8,128)S(1)}, f32[5,512,1024]{2,1,0:T(8,128)}) fusion(f32[5,512,1024]{2,1,0:T(8,128)} %get-tuple-element.164, f32[5,512]{1,0:T(8,128)S(1)} %log_add_fusion.4, pred[512,1024]{1,0:T(8,128)(4,1)S(1)} %copy-done.16, bf16[3072,5,3,24]{0,3,1,2:T(8,128)(2,1)} %copy-done.26, bf16[3072,5,24]{0,2,1:T(8,128)(2,1)} %copy-done.24), kind=kOutput, calls=%fused_computation.14 | convolution fusion | flops 136312320 | bytes 21884928 | tf_op jit(solution)/shard_map/qhd,khd->hqk/dot_general | solution.py:247
  397.1 8.4 %multiply_reduce_fusion.5 = (f32[5,512]{1,0:T(8,128)S(1)}, f32[5,512,1024]{2,1,0:T(8,128)}) fusion(f32[5,512,1024]{2,1,0:T(8,128)S(1)} %bitcast.195, f32[5,512]{1,0:T(8,128)S(1)} %log_add_fusion.5, pred[512,1024]{1,0:T(8,128)(4,1)S(1)} %copy-done.14, bf16[3072,5,3,24]{0,3,1,2:T(8,128)(2,1)} %copy-done.26, bf16[3072,5,24]{0,2,1:T(8,128)(2,1)} %copy-done.24), kind=kOutput, calls=%fused_computation.17 | convolution fusion | flops 136312320 | bytes 21884928 | tf_op jit(solution)/shard_map/qhd,khd->hqk/dot_general | solution.py:247
  405.5 15.1 %multiply_convert_fusion.4 = (bf16[5,512,1024]{2,1,0:T(8,128)(2,1)}, bf16[5,512,1024]{2,1,0:T(8,128)(2,1)}) fusion(f32[5,512,1024]{2,1,0:T(8,128)} %get-tuple-element.186, f32[5,512,1024]{2,1,0:T(8,128)} %get-tuple-element.164, f32[5,512]{1,0:T(8,128)S(1)} %get-tuple-element.185, f32[5,512]{1,0:T(8,128)S(1)} %log_add_fusion.4, ...), kind=kLoop, calls=%fused_computation.13 | loop fusion | flops 26214400 | bytes 53518336 | tf_op jit(solution)/shard_map/convert_element_type | solution.py:251
  433.3 7.4 %multiply_reduce_fusion.3 = (f32[5,512]{1,0:T(8,128)S(1)}, f32[5,512,1024]{2,1,0:T(8,128)}) fusion(f32[5,512,1024]{2,1,0:T(8,128)S(1)} %bitcast.193, f32[5,512]{1,0:T(8,128)S(1)} %log_add_fusion.3, pred[512,1024]{1,0:T(8,128)(4,1)S(1)} %copy-done.10, bf16[3072,5,3,24]{0,3,1,2:T(8,128)(2,1)} %copy-done.26, bf16[3072,5,24]{0,2,1:T(8,128)(2,1)S(1)} %copy-done.25), kind=kOutput, calls=%fused_computation.11 | convolution fusion | flops 136312320 | bytes 21891072 | tf_op jit(solution)/shard_map/qhd,khd->hqk/dot_general | solution.py:247
  444.0 9.4 %multiply_reduce_fusion.1 = (f32[5,512]{1,0:T(8,128)S(1)}, f32[5,512,1024]{2,1,0:T(8,128)}) fusion(f32[5,512,1024]{2,1,0:T(8,128)} %get-tuple-element.170, f32[5,512]{1,0:T(8,128)S(1)} %log_add_fusion.1, pred[512,1024]{1,0:T(8,128)(4,1)S(1)} %copy-done.12, bf16[3072,5,3,24]{0,3,1,2:T(8,128)(2,1)} %copy-done.26, bf16[3072,5,24]{0,2,1:T(8,128)(2,1)S(1)} %copy-done.25), kind=kOutput, calls=%fused_computation.5 | convolution fusion | flops 136312320 | bytes 21891072 | tf_op jit(solution)/shard_map/qhd,khd->hqk/dot_general | solution.py:247
  459.5 15.0 %multiply_convert_fusion = (bf16[5,512,1024]{2,1,0:T(8,128)(2,1)}, bf16[5,512,1024]{2,1,0:T(8,128)(2,1)}) fusion(f32[5,512,1024]{2,1,0:T(8,128)} %get-tuple-element.178, f32[5,512,1024]{2,1,0:T(8,128)S(1)} %bitcast.191, f32[5,512]{1,0:T(8,128)S(1)} %get-tuple-element.177, f32[5,512]{1,0:T(8,128)S(1)} %log_add_fusion, ...), kind=kLoop, calls=%fused_computation.1 | loop fusion | flops 26214400 | bytes 53518336 | tf_op jit(solution)/shard_map/convert_element_type | solution.py:251
  478.1 14.0 %multiply_convert_fusion.2 = (bf16[5,512,1024]{2,1,0:T(8,128)(2,1)S(1)}, bf16[5,512,1024]{2,1,0:T(8,128)(2,1)}) fusion(f32[5,512,1024]{2,1,0:T(8,128)} %get-tuple-element.182, f32[5,512,1024]{2,1,0:T(8,128)S(1)} %bitcast.187, f32[5,512]{1,0:T(8,128)S(1)} %get-tuple-element.181, f32[5,512]{1,0:T(8,128)S(1)} %log_add_fusion.2, ...), kind=kLoop, calls=%fused_computation.7 | loop fusion | flops 26214400 | bytes 53518336 | tf_op jit(solution)/shard_map/convert_element_type | solution.py:251
  525.9 7.5 %convert_element_type.196 = bf16[3,1024,360]{1,0,2:T(4,128)(2,1)} reshape(bf16[3072,5,3,24]{0,3,2,1:T(8,128)(2,1)} %copy-done.8) | data formatting | bytes 4423680 | tf_op jit(solution)/shard_map/convert_element_type | solution.py:271
  549.9 22.0 %psum.73 = f32[360]{0:T(512)} all-reduce(f32[360]{0:T(512)S(1)} %reduce_sum.339), channel_id=1, replica_groups=mesh['dp'=8,'heads'=4] {'dp'}, use_global_device_ids=true, to_apply=%region_38.39 | all-reduce | flops 360 | bytes 2880 | tf_op jit(solution)/shard_map/psum | solution.py:292
  577.2 37.6 %all-reduce.8 = (f32[480]{0:T(512)}, f32[480]{0:T(512)}, f32[480]{0:T(512)}, f32[480]{0:T(512)}, f32[480]{0:T(512)}, /*index=5*/f32[1920]{0:T(1024)}, f32[480]{0:T(512)}) all-reduce(f32[480]{0:T(512)S(1)} %get-tuple-element.100, f32[480]{0:T(512)S(1)} %get-tuple-element.103, ...), channel_id=1, replica_groups=mesh['dp'=8,'heads'=4] {'dp','heads'}, use_global_device_ids=true, to_apply=%region_33.34 | all-reduce | flops 4800 | bytes 38400 | tf_op jit(solution)/shard_map/psum | solution.py:296
  617.7 22.7 %all-reduce.12.cloned.1.call-done = (f32[480,360]{1,0:T(8,128)}, f32[120,480]{1,0:T(8,128)}) async-done(((f32[480,360]{1,0:T(8,128)}, f32[120,480]{1,0:T(8,128)}), (f32[480,360]{1,0:T(8,128)}, f32[120,480]{1,0:T(8,128)})) %all-reduce.12.cloned.1.call-update) | async-done | bytes 921616 | tf_op jit(solution)/shard_map/psum | solution.py:292
  640.4 66.5 %reduce-scatter.21.cloned.1.call-done = f32[240,120]{1,0:T(8,128)} async-done(((f32[1920,120]{1,0:T(8,128)}), f32[240,120]{1,0:T(8,128)}) %reduce-scatter.21.cloned.1.call-update) | async-done | bytes 115216
  (382 shorter events, 215.5 us)
Async XLA Ops:
  7.2 37.4 %all-gather.5.cloned.1.call-start = ((), (), s32[]{:S(2)}) async-start(), calls=%async_computation.6 | async-start | bytes 3686400 | tf_op jit(solution)/shard_map/all_gather | solution.py:118
  14.0 224.7 %reduce-scatter.15.cloned.1.call-start = ((), (), s32[]{:S(2)}) async-start(), calls=%async_computation.7 | async-start | bytes 7372800 | tf_op jit(solution)/shard_map/reduce_scatter | solution.py:176
  15.1 130.8 %copy-start.9 = (pred[512,1024]{1,0:T(8,128)(4,1)}, pred[512,1024]{1,0:T(8,128)(4,1)S(1)}, u32[]{:S(2)}) copy-start(pred[512,1024]{1,0:T(8,128)(4,1)S(1)} %get-tuple-element.158) | copy-start | bytes 1572868
  15.8 139.6 %copy-start.11 = (pred[512,1024]{1,0:T(8,128)(4,1)}, pred[512,1024]{1,0:T(8,128)(4,1)S(1)}, u32[]{:S(2)}) copy-start(pred[512,1024]{1,0:T(8,128)(4,1)S(1)} %get-tuple-element.156) | copy-start | bytes 1572868
  17.2 107.2 %copy-start.13 = (pred[512,1024]{1,0:T(8,128)(4,1)}, pred[512,1024]{1,0:T(8,128)(4,1)S(1)}, u32[]{:S(2)}) copy-start(pred[512,1024]{1,0:T(8,128)(4,1)S(1)} %get-tuple-element.160) | copy-start | bytes 1572868
  18.0 47.9 %copy-start.40 = (f32[3072,12]{0,1:T(8,128)}, f32[3072,12]{0,1:T(8,128)S(1)}, u32[]{:S(2)}) copy-start(f32[3072,12]{0,1:T(8,128)S(1)} %get-tuple-element.153) | copy-start | bytes 442372
  18.0 47.9 %copy-start.42 = (f32[3072,12]{0,1:T(8,128)}, f32[3072,12]{0,1:T(8,128)S(1)}, u32[]{:S(2)}) copy-start(f32[3072,12]{0,1:T(8,128)S(1)} %get-tuple-element.154) | copy-start | bytes 442372
  65.6 96.1 %copy-start.26 = (bf16[3072,5,3,24]{0,3,1,2:T(8,128)(2,1)}, bf16[3072,5,3,24]{0,3,1,2:T(8,128)(2,1)S(1)}, u32[]{:S(2)}) copy-start(bf16[3072,5,3,24]{0,3,1,2:T(8,128)(2,1)S(1)} %copy.146) | copy-start | bytes 6635524
  91.5 60.5 %copy-start.2 = (f32[5,512,1024]{2,1,0:T(8,128)}, f32[5,512,1024]{2,1,0:T(8,128)S(1)}, u32[]{:S(2)}) copy-start(f32[5,512,1024]{2,1,0:T(8,128)S(1)} %get-tuple-element.168) | copy-start | bytes 31457284
  97.6 48.4 %copy-start.53 = (f32[5,512]{1,0:T(8,128)}, f32[5,512]{1,0:T(8,128)S(1)}, u32[]{:S(2)}) copy-start(f32[5,512]{1,0:T(8,128)S(1)} %get-tuple-element.165) | copy-start | bytes 30724
  104.7 56.9 %copy-start.67 = (f32[5,512]{1,0:T(8,128)}, f32[5,512]{1,0:T(8,128)S(1)}, u32[]{:S(2)}) copy-start(f32[5,512]{1,0:T(8,128)S(1)} %fusion.5) | copy-start | bytes 30724
  171.9 65.8 %copy-start.87 = (s32[3,4]{1,0:T(4,128)S(1)}, s32[3,4]{1,0:T(4,128)}, u32[]{:S(2)}) copy-start(s32[3,4]{1,0:T(4,128)} %param.31) | copy-start | bytes 148
  171.9 65.9 %copy-start.1 = (f32[1024]{0:T(1024)S(1)}, f32[1024]{0:T(1024)}, u32[]{:S(2)}) copy-start(f32[1024]{0:T(1024)} %param.32) | copy-start | bytes 12292
  171.9 66.8 %copy-start.4 = (bf16[768,480]{0,1:T(8,128)(2,1)S(1)}, bf16[768,480]{0,1:T(8,128)(2,1)}, u32[]{:S(2)}) copy-start(bf16[768,480]{0,1:T(8,128)(2,1)} %param.17) | copy-start | bytes 2211844
  171.9 66.8 %copy-start.83 = (f32[480]{0:T(512)S(1)}, f32[480]{0:T(512)}, u32[]{:S(2)}) copy-start(f32[480]{0:T(512)} %param.23) | copy-start | bytes 5764
  172.0 79.3 %all-gather.7.cloned.1.call-start = ((), (), s32[]{:S(2)}) async-start(), calls=%async_computation.8 | async-start | bytes 2304000 | tf_op jit(solution)/shard_map/all_gather | solution.py:192
  204.3 46.9 %copy-start.88 = (f32[1920]{0:T(1024)S(1)}, f32[1920]{0:T(1024)}, u32[]{:S(2)}) copy-start(f32[1920]{0:T(1024)} %param.27) | copy-start | bytes 23044
  204.3 46.9 %copy-start.89 = (f32[480]{0:T(512)S(1)}, f32[480]{0:T(512)}, u32[]{:S(2)}) copy-start(f32[480]{0:T(512)} %param.25) | copy-start | bytes 5764
  205.4 68.6 %all-gather.9.cloned.1.call-start = ((), (), s32[]{:S(2)}) async-start(), calls=%async_computation.9 | async-start | bytes 2304000 | tf_op jit(solution)/shard_map/all_gather | solution.py:193
  237.7 79.2 %reduce-scatter.23.cloned.1.call-start = ((), (), s32[]{:S(2)}) async-start(), calls=%async_computation.14 | async-start | bytes 2304000
  238.7 59.8 %copy-start.71 = (f32[768]{0:T(1024)}, f32[768]{0:T(1024)S(1)}, u32[]{:S(2)}) copy-start(f32[768]{0:T(1024)S(1)} %mul.361) | copy-start | bytes 9220
  286.8 60.0 %all-gather.11.cloned.1.call-start = ((), (), s32[]{:S(2)}) async-start(), calls=%async_computation.10 | async-start | bytes 3686400 | tf_op jit(solution)/shard_map/all_gather | solution.py:216
  298.4 243.4 %reduce-scatter.25.cloned.1.call-start = ((), (), s32[]{:S(2)}) async-start(), calls=%async_computation.15 | async-start | bytes 2304000
  298.6 48.2 %copy-start.48 = (bf16[120,480]{1,0:T(8,128)(2,1)S(1)}, bf16[120,480]{1,0:T(8,128)(2,1)}, u32[]{:S(2)}) copy-start(bf16[120,480]{1,0:T(8,128)(2,1)} %param.22) | copy-start | bytes 345604
  303.4 268.4 %reduce-scatter.19.cloned.1.call-start = ((), (), s32[]{:S(2)}) async-start(), calls=%async_computation.12 | async-start | bytes 1105920
  319.1 254.4 %reduce-scatter.17.cloned.1.call-start = ((), (), s32[]{:S(2)}) async-start(), calls=%async_computation.11 | async-start | bytes 3686400 | tf_op jit(solution)/shard_map/reduce_scatter | solution.py:284
  522.2 118.2 %all-reduce.12.cloned.1.call-start = ((), (), s32[]{:S(2)}) async-start(), calls=%async_computation.16 | async-start | bytes 1966080 | tf_op jit(solution)/shard_map/psum | solution.py:292
  541.8 165.2 %reduce-scatter.21.cloned.1.call-start = ((), (), s32[]{:S(2)}) async-start(), calls=%async_computation.13 | async-start | bytes 1105920
  544.2 70.6 %copy-start.18 = (f32[768,480]{0,1:T(8,128)S(1)}, f32[768,480]{0,1:T(8,128)}, u32[]{:S(2)}) copy-start(f32[768,480]{0,1:T(8,128)} %copy-done.17) | copy-start | bytes 4423684
  544.2 70.6 %copy-start.35 = (bf16[768,480]{0,1:T(8,128)(2,1)S(1)}, bf16[768,480]{0,1:T(8,128)(2,1)}, u32[]{:S(2)}) copy-start(bf16[768,480]{0,1:T(8,128)(2,1)} %param.33) | copy-start | bytes 2211844
  544.2 70.5 %copy-start.72 = (f32[768]{0:T(1024)S(1)}, f32[768]{0:T(1024)}, u32[]{:S(2)}) copy-start(f32[768]{0:T(1024)} %copy-done.71) | copy-start | bytes 9220
  544.2 70.5 %copy-start.74 = (f32[768]{0:T(1024)S(1)}, f32[768]{0:T(1024)}, u32[]{:S(2)}) copy-start(f32[768]{0:T(1024)} %copy-done.73) | copy-start | bytes 9220
  (94 other events, 1178.6 us)
Sparse Core Ops, SparseCore 0:
  14.1 30.4 all-gather.4
  172.1 55.7 reduce-scatter.14
  230.1 21.1 all-gather.6
  252.8 21.1 all-gather.8
  286.9 29.9 reduce-scatter.22
  318.9 27.7 all-gather.10
  349.5 29.9 reduce-scatter.24
  383.2 63.3 reduce-scatter.18
  522.3 36.7 reduce-scatter.16
  563.4 77.0 all-reduce.11
  644.7 62.1 reduce-scatter.20
where the time goes:
time: 726 us; the launch traced here: 717 us
  matrix products  238 us (33%)
  waiting for transfers between devices  171 us (24%)
  blocking collectives  122 us (17%)
  other arithmetic  101 us (14%)
  local copies, waits for them, and re-layouts  69.1 us (10%)
  between operations  15.7 us (2%)
    unnamed x15, waiting for transfers between devices  79.9 us
    dot_general x6, matrix products, local(): jnp.einsum('qhd,khd->hqk', grad_block, group_values, preferred_element_ty...  52 us
    convert_element_type x3, other arithmetic, local(): d_scores = (prob_full * (d_prob - row_inner)).astype(jnp.bfloat16)  44.1 us
    psum x1, blocking collectives, local(): lax.psum((d_attn_gain, d_attn_shift, d_out_bias, d_ffn_gain, d_ffn_shift,...  37.6 us
    reduce_sum x6, other arithmetic, local(): denominator = jnp.sum(exp_terms, axis=-1, keepdims=True)  35.6 us
    dot_general x6, matrix products, local(): jnp.einsum('hqk,qhd->khd', weights_low, grad_block, preferred_element_typ...  32.3 us
    all_gather x1, blocking collectives, local(): lax.all_gather(up_weight, 'dp', axis=1, tiled=True)  31.5 us
    dot_general x6, matrix products, local(): jnp.einsum('hqk,khd->qhd', weights_low, group_values, preferred_element_t...  31.5 us
  transfers between devices with their start and end apart: 11, of which 7 were waited for; matrix products, arithmetic and copies ran while one was open for 35% of the time, Pallas kernels for 0%

commit v1 on v0

v1 whole, which is shorter than its diff:
```python
from functools import partial

import jax
import jax.numpy as jnp
import numpy as np
from jax import lax
from jax.experimental import pallas as pl
from jax.experimental.pallas import tpu as pltpu
from jax.sharding import PartitionSpec as P

F32, BF16 = jnp.float32, jnp.bfloat16
MESH = pl.DeviceIdType.MESH
HD = 24
HEADS = 5
USED = HEADS * HD
LANES = 128
EPSILON = 1e-05
LOG2E = 1.4426950408889634
BIG = 1e30
BLOCK = 256
FF_TILE = 384


def dims(a, b, ca, cb, precision=None):
    return lax.dot_general(
        a, b, (((ca,), (cb,)), ((), ())), preferred_element_type=F32, precision=precision
    )


def nn(a, b):
    return dims(a, b, 1, 0)


def nt(a, b):
    return dims(a, b, 1, 1)


def tn(a, b):
    return dims(a, b, 0, 0)


def lane(rows, width=LANES):
    return lax.broadcasted_iota(jnp.int32, (rows, width), 1)


def head_lanes(rows, j):
    at = lane(rows)
    return (at >= HD * j) & (at < HD * (j + 1))


def partner(x):
    at = lane(x.shape[0])
    half = HD // 2
    return jnp.where(
        at % HD < half, pltpu.roll(x, LANES - half, 1), pltpu.roll(x, half, 1)
    )


def norm(x):
    centred = x - jnp.mean(x, axis=-1, keepdims=True)
    rstd = lax.rsqrt(jnp.mean(centred * centred, axis=-1, keepdims=True) + EPSILON)
    return centred * rstd, rstd


def norm_back(g, gain, xhat, rstd):
    n = g * gain
    return rstd * (
        n
        - jnp.mean(n, axis=-1, keepdims=True)
        - xhat * jnp.mean(n * xhat, axis=-1, keepdims=True)
    )


def body(
    tok, grad, wqkv, wout, upt, down, attn_gain, attn_bias, qkv_bias, out_bias, ffn_gain,
    ffn_bias, up_bias, down_bias, perm, cos, sin, lengths, ids, cw,
    result, dtok, dwqkv, dwout, dup, ddown, sums, dupb, dqkvb, phbm,
    n1, wq, wo, qkv_b, q_s, k_s, v_s, ctx, ctxb, invl, pslot,
    rs_core_out, rs_core_in, rs_y_out, rs_y_in, rs_own,
    mid, n2, df, facc, dn2, gup, gdown, da, do_s, dot_t, q_t, dq, dk_t, dv_t, dqkv,
    ag_s, ag_r, rs_s, rs_r, p_s,
):
    d, h = lax.axis_index("dp"), lax.axis_index("heads")
    core, y = h % 2, h // 2
    h_sib = h + 1 - 2 * core
    h_y = (h + 2) % 4
    sib, ypart = (d, h_sib), (d, h_y)
    groups = lengths.shape[0]
    width = tok.shape[1]
    group_rows = 4 * BLOCK
    steps = 4

    def send(src, dst, s, r, to):
        return pltpu.make_async_remote_copy(
            src_ref=src, dst_ref=dst, send_sem=s, recv_sem=r, device_id=to, device_id_type=MESH
        )

    def gather_copy(use, buf, k, n):
        block, to = ((h, sib), (h, ypart), (h_y, sib))[n]
        return send(
            buf.at[k, block], buf.at[k, block], ag_s.at[use, k, n], ag_r.at[use, k, n], to
        )

    def gather_start(use, buf, k):
        gather_copy(use, buf, k, 1).start()
        gather_copy(use, buf, k, 0).start()

    def gather_forward(use, buf, k):
        gather_copy(use, buf, k, 1).wait_recv()
        gather_copy(use, buf, k, 2).start()

    def gather_finish(use, buf, k):
        gather_copy(use, buf, k, 0).wait_recv()
        gather_copy(use, buf, k, 2).wait_recv()

    def gather_sent(use, buf, k):
        for n in range(3):
            gather_copy(use, buf, k, n).wait_send()

    def sum_copy(use, k, n):
        src, dst, to = ((rs_core_out, rs_core_in, sib), (rs_y_out, rs_y_in, ypart))[n]
        return send(src.at[k], dst.at[k], rs_s.at[use, k, n], rs_r.at[use, k, n], to)

    def sum_start(use, k, part):
        for other in (0, 1):
            rs_core_out[k, other] = part(2 * other + 1 - core).astype(BF16)
        sum_copy(use, k, 0).start()
        for other in (0, 1):
            rs_own[k, other] = part(2 * other + core)

    def sum_forward(use, k):
        sum_copy(use, k, 0).wait_recv()
        rs_y_out[k] = (rs_own[k, 1 - y] + rs_core_in[k, 1 - y].astype(F32)).astype(BF16)
        sum_copy(use, k, 1).start()

    def sum_finish(use, k):
        sum_copy(use, k, 1).wait_recv()
        return rs_own[k, y] + rs_core_in[k, y].astype(F32) + rs_y_in[k].astype(F32)

    def sum_sent(use, k):
        for n in range(2):
            sum_copy(use, k, n).wait_send()

    def rows_of(k):
        return slice(k * BLOCK, (k + 1) * BLOCK)

    def add_sum(row, value):
        sums[row : row + 1, 0:width] += value

    barrier = pltpu.get_barrier_semaphore()
    for other in (sib, ypart):
        pl.semaphore_signal(barrier, inc=1, device_id=other, device_id_type=MESH)

    def first_norm(k):
        xhat, _ = norm(tok[rows_of(k), :].astype(F32))
        n1[k, h, :, 0:width] = (xhat * attn_gain[...] + attn_bias[...]).astype(BF16)
        n1[k, h, :, width:512] = jnp.zeros((BLOCK, 512 - width), BF16)

    first_norm(0)
    pl.semaphore_wait(barrier, 2)
    gather_start(0, n1, 0)
    for k in range(1, groups):
        first_norm(k)
        gather_start(0, n1, k)

    wq[0:width, :] = nn(wqkv[...], perm[...]).astype(BF16)
    wq[width:512, :] = jnp.zeros((512 - width, 3 * LANES), BF16)
    qkv_b[...] = dims(qkv_bias[...], perm[...].astype(F32), 1, 0, lax.Precision.HIGHEST)
    wo[:, width:512] = jnp.zeros((LANES, 512 - width), BF16)
    wo[:, 0:width] = jnp.concatenate(
        [wout[...].astype(F32), jnp.zeros((LANES - USED, width), F32)], axis=0
    ).astype(BF16)
    sums[...] = jnp.zeros_like(sums)
    dwqkv[...] = jnp.zeros_like(dwqkv)
    dwout[...] = jnp.zeros_like(dwout)
    dqkvb[...] = jnp.zeros_like(dqkvb)
    dupb[...] = jnp.zeros_like(dupb)
    n2[:, width:512] = jnp.zeros((groups * BLOCK, 512 - width), BF16)
    df[:, width:512] = jnp.zeros((groups * BLOCK, 512 - width), BF16)
    for k in range(groups):
        da[k, h, :, width:512] = jnp.zeros((BLOCK, 512 - width), BF16)

    def ends_of(k):
        total, ends = 0, []
        for p in range(4):
            total = total + lengths[k, p]
            ends.append(total)
        return ends

    def project(k):
        ends = ends_of(k)
        at1 = lane(1)
        lo = jnp.where(at1 == USED, 0, group_rows + 1)
        hi = jnp.where(at1 == USED + 4, group_rows + 1, 0)
        for p in range(4):
            lo = jnp.where(at1 == USED + 1 + p, ends[p], lo)
            hi = jnp.where(at1 == USED + p, ends[p], hi)

        def step(i, _):
            r = pl.ds(pl.multiple_of(i * BLOCK, BLOCK), BLOCK)
            x = nn(n1[k, i], wq[...]) + qkv_b[...]
            c, s = cos[r, :], sin[r, :]
            at = lane(BLOCK)
            row = lax.broadcasted_iota(jnp.int32, (BLOCK, LANES), 0) + i * BLOCK
            inside = (row >= lo) & (row < hi)
            marks = (at >= USED) & (at < USED + 5)
            q = x[:, 0:LANES]
            q = (q * c + partner(q) * s) * (HD ** (-0.5) * LOG2E)
            q_s[k, r, :] = jnp.where(at < USED, q, jnp.where(inside, 1.0, 0.0)).astype(BF16)
            key = x[:, LANES : 2 * LANES]
            key = key * c + partner(key) * s
            k_s[k, r, :] = jnp.where(
                at < USED, key, jnp.where(marks & jnp.logical_not(inside), -BIG, 0.0)
            ).astype(BF16)
            v_s[k, r, :] = jnp.where(
                at < USED, x[:, 2 * LANES : 3 * LANES], jnp.where(at < USED + 2, 1.0, 0.0)
            ).astype(BF16)
            return 0

        lax.fori_loop(0, steps, step, 0)

    def p_out(k, i):
        slot = (k * steps + i) % 2
        return pltpu.make_async_copy(pslot.at[slot], phbm.at[k, i], p_s.at[slot])

    def p_in(n):
        slot = n % 2
        return pltpu.make_async_copy(phbm.at[n // steps, n % steps], pslot.at[slot], p_s.at[slot])

    def attend(k, first, last):
        def step(i, _):
            n = k * steps + i
            slot = n % 2

            @pl.when(n >= 2)
            def _():
                p_out(k, i).wait()

            r = pl.ds(pl.multiple_of(i * BLOCK, BLOCK), BLOCK)
            q = q_s[k, r, :]
            keys, vals = k_s[k], v_s[k]
            at = lane(BLOCK)

            def score(j):
                return nt(jnp.where(head_lanes(BLOCK, j) | (at >= USED), q, 0), keys)

            acc = jnp.zeros((BLOCK, LANES), F32)
            inv = jnp.zeros((BLOCK, LANES), F32)
            s = score(0)
            for j in range(HEADS):
                later = score(j + 1) if j + 1 < HEADS else None
                e = jnp.exp2(s - jnp.max(s, axis=1, keepdims=True)).astype(BF16)
                pslot[slot, j] = e
                o = nn(e, vals)
                one = 1.0 / o[:, USED : USED + 1]
                acc = jnp.where(head_lanes(BLOCK, j), o * one, acc)
                inv = jnp.where(head_lanes(BLOCK, j), one, inv)
                s = later
            ctx[k, r, :] = acc
            ctxb[k, r, :] = acc.astype(BF16)
            invl[k, r, :] = inv
            p_out(k, i).start()
            return 0

        lax.fori_loop(first, last, step, 0)

    def out_part(k):
        def part(i):
            r = pl.ds(pl.multiple_of(i * BLOCK, BLOCK), BLOCK)
            return nn(ctxb[k, r, :], wo[...])

        return part

    gather_forward(0, n1, 0)
    for k in range(groups):
        gather_finish(0, n1, k)
        project(k)
        if k > 0:
            sum_forward(0, k - 1)
        attend(k, 0, steps - 1)
        if k + 1 < groups:
            gather_forward(0, n1, k + 1)
        attend(k, steps - 1, steps)
        sum_start(0, k, out_part(k))
    sum_forward(0, groups - 1)
    for n in (groups * steps, groups * steps + 1):
        p_in(n % 2).wait()
    p_in(0).start()
    p_in(1).start()

    def weight_of(k):
        ends = ends_of(k)
        row = lax.broadcasted_iota(jnp.int32, (BLOCK, 1), 0) + h * BLOCK
        w = jnp.zeros((BLOCK, 1), F32)
        for p in reversed(range(4)):
            w = jnp.where(row < ends[p], cw[ids[k, p]], w)
        return w

    def ffn_pre(k):
        r = rows_of(k)
        middle = tok[r, :].astype(F32) + sum_finish(0, k)[:, 0:width] + out_bias[...]
        mid[r, :] = middle
        xhat, _ = norm(middle)
        n2[r, 0:width] = (xhat * ffn_gain[...] + ffn_bias[...]).astype(BF16)
        d_ffn = (grad[r, :].astype(F32) * weight_of(k)).astype(BF16)
        df[r, 0:width] = d_ffn
        add_sum(5, jnp.sum(d_ffn.astype(F32), axis=0, keepdims=True))

    def ffn_core(first, last):
        r = slice(first * BLOCK, last * BLOCK)

        def step(t, _):
            f = pl.ds(pl.multiple_of(t * FF_TILE, FF_TILE), FF_TILE)
            wu, wd = upt[f, :], down[f, :]
            x, g = n2[r, :], df[r, :]
            u = nt(x, wu) + up_bias[:, f]
            phi = 0.5 + 0.5 * lax.erf(u * (0.5**0.5))
            hid = (u * phi).astype(BF16)
            slope = phi + u * (jnp.exp(u * u * -0.5) * 0.3989422804014327)
            out = nn(hid, wd)
            du = (nt(g, wd) * slope).astype(BF16)
            dx = nn(du, wu)
            gu, gd = tn(du, x), tn(hid, g)
            dupb[:, f] += jnp.sum(du.astype(F32), axis=0, keepdims=True)

            @pl.when(t == 0)
            def _():
                facc[r, :] = out
                dn2[r, :] = dx

            @pl.when(t > 0)
            def _():
                facc[r, :] += out
                dn2[r, :] += dx

            if first == 0:
                gup[f, :] = gu
                gdown[f, :] = gd
            else:
                gup[f, :] += gu
                gdown[f, :] += gd
            return 0

        lax.fori_loop(0, upt.shape[0] // FF_TILE, step, 0)

    def ffn_post(k):
        r = rows_of(k)
        middle = mid[r, :]
        result[r, :] = (middle + facc[r, 0:width] + down_bias[...]).astype(BF16)
        g = dn2[r, 0:width]
        xhat, rstd = norm(middle)
        add_sum(3, jnp.sum(g * xhat, axis=0, keepdims=True))
        add_sum(4, jnp.sum(g, axis=0, keepdims=True))
        d_result = grad[r, :].astype(F32) * weight_of(k)
        d_middle = d_result + norm_back(g, ffn_gain[...], xhat, rstd)
        dtok[r, :] = d_middle
        low = d_middle.astype(BF16)
        da[k, h, :, 0:width] = low
        add_sum(2, jnp.sum(low.astype(F32), axis=0, keepdims=True))
        gather_start(1, da, k)

    for k in range(groups - 1):
        ffn_pre(k)
    ffn_core(0, groups - 1)
    for k in range(groups - 1):
        ffn_post(k)
    ffn_pre(groups - 1)
    ffn_core(groups - 1, groups)
    ffn_post(groups - 1)
    dup[...] = gup[...].astype(BF16)
    ddown[...] = gdown[...].astype(BF16)
    for k in range(groups):
        gather_sent(0, n1, k)
        sum_sent(0, k)

    def back_prep(k):
        def step(i, _):
            r = pl.ds(pl.multiple_of(i * BLOCK, BLOCK), BLOCK)
            g = nt(da[k, i], wo[...]).astype(BF16).astype(F32)
            g = (g * invl[k, r, :]).astype(BF16)
            do_s[r, :] = g
            dot_t[:, r] = g.astype(F32).T
            q_t[:, r] = q_s[k, r, :].astype(F32).T
            dwout[...] += tn(ctxb[k, r, :], da[k, i])
            return 0

        lax.fori_loop(0, steps, step, 0)
        dk_t[...] = jnp.zeros_like(dk_t)
        dv_t[...] = jnp.zeros_like(dv_t)

    def back(k, first, last):
        def step(i, _):
            n = k * steps + i
            slot = n % 2
            p_in(n).wait()
            r = pl.ds(pl.multiple_of(i * BLOCK, BLOCK), BLOCK)
            g = do_s[r, :].astype(F32)
            prod = g * ctx[k, r, :]
            keys, vals = k_s[k], v_s[k]
            at = lane(BLOCK)

            def d_prob(j):
                mine = head_lanes(BLOCK, j)
                inner = jnp.sum(jnp.where(mine, prod, 0.0), axis=1, keepdims=True)
                top = inner.astype(BF16).astype(F32)
                row = jnp.where(at == USED, -top, jnp.where(at == USED + 1, top - inner, 0.0))
                return nt(jnp.where(mine, g, row).astype(BF16), vals)

            acc = jnp.zeros((BLOCK, LANES), F32)
            dp = d_prob(0)
            for j in range(HEADS):
                later = d_prob(j + 1) if j + 1 < HEADS else None
                e = pslot[slot, j]
                ds = (e.astype(F32) * dp).astype(BF16)
                acc = jnp.where(head_lanes(BLOCK, j), nn(ds, keys), acc)
                hs = slice(j * HD, (j + 1) * HD)
                dk_t[hs, :] += nn(q_t[hs, r].astype(BF16), ds)
                dv_t[hs, :] += nn(dot_t[hs, r].astype(BF16), e)
                dp = later
            dq[r, :] = acc

            @pl.when(n + 2 < groups * steps)
            def _():
                p_in(n + 2).start()

            return 0

        lax.fori_loop(first, last, step, 0)

    def back_post(k):
        def step(i, _):
            r = pl.ds(pl.multiple_of(i * BLOCK, BLOCK), BLOCK)
            c, s = cos[r, :], sin[r, :]
            a = dq[r, :] * HD ** (-0.5)
            a = a * c - partner(a) * s
            b = dk_t[:, r].T * (1.0 / LOG2E)
            b = b * c - partner(b) * s
            g = jnp.concatenate([a, b, dv_t[:, r].T], axis=1).astype(BF16)
            dqkv[r, :] = g
            dqkvb[...] += jnp.sum(g.astype(F32), axis=0, keepdims=True)
            dwqkv[...] += tn(g, n1[k, i])
            return 0

        lax.fori_loop(0, steps, step, 0)

    def tokens_part(i):
        r = pl.ds(pl.multiple_of(i * BLOCK, BLOCK), BLOCK)
        return nt(dqkv[r, :], wq[...])

    def last_norm(k):
        r = rows_of(k)
        g = sum_finish(1, k)[:, 0:width]
        xhat, rstd = norm(tok[r, :].astype(F32))
        add_sum(0, jnp.sum(g * xhat, axis=0, keepdims=True))
        add_sum(1, jnp.sum(g, axis=0, keepdims=True))
        dtok[r, :] += norm_back(g, attn_gain[...], xhat, rstd)

    for k in range(groups - 1):
        gather_forward(1, da, k)
    for k in range(groups):
        gather_finish(1, da, k)
        back_prep(k)
        if k > 0:
            sum_forward(1, k - 1)
        if k == 0:
            back(k, 0, 1)
            gather_forward(1, da, groups - 1)
            back(k, 1, steps)
        else:
            back(k, 0, steps)
        back_post(k)
        sum_start(1, k, tokens_part)
    for k in range(groups - 1):
        last_norm(k)
    sum_forward(1, groups - 1)
    last_norm(groups - 1)
    for k in range(groups):
        gather_sent(1, da, k)
        sum_sent(1, k)


def permutation():
    table = np.zeros((3 * USED, 3 * LANES), np.float32)
    for j in range(HEADS):
        for part in range(3):
            for i in range(HD):
                table[(j * 3 + part) * HD + i, part * LANES + j * HD + i] = 1.0
    return table


def turns(group_rows):
    freq = 10000.0 ** (-2.0 * np.arange(HD // 2) / HD)
    angle = np.arange(group_rows)[:, None] * freq[None, :]
    c = np.zeros((group_rows, LANES), np.float32)
    s = np.zeros((group_rows, LANES), np.float32)
    c[:, :USED] = np.tile(np.cos(angle), (1, 2 * HEADS))
    s[:, :USED] = np.tile(np.concatenate([-np.sin(angle), np.sin(angle)], axis=1), (1, HEADS))
    return c, s


def layer(
    tokens, wqkv, wout, upt, down, attn_gain, attn_bias, qkv_bias, out_bias, ffn_gain,
    ffn_bias, up_bias, down_bias, lengths, ids, cw, grad,
):
    own, width = tokens.shape
    groups = lengths.shape[0]
    ff = up_bias.shape[0]
    group_rows = 4 * BLOCK
    c, s = turns(group_rows)
    vm = pl.BlockSpec(memory_space=pltpu.VMEM)
    sm = pl.BlockSpec(memory_space=pltpu.SMEM)
    anywhere = pl.BlockSpec(memory_space=pl.ANY)
    shape = jax.ShapeDtypeStruct
    row = lambda v: v.reshape(1, -1)
    v, dma = pltpu.VMEM, pltpu.SemaphoreType.DMA
    return pl.pallas_call(
        body,
        out_shape=(
            shape((own, width), BF16),
            shape((own, width), F32),
            shape((3 * LANES, 512), F32),
            shape((LANES, 512), F32),
            shape((ff, 512), BF16),
            shape((ff, 512), BF16),
            shape((8, 512), F32),
            shape((1, ff), F32),
            shape((1, 3 * LANES), F32),
            shape((groups, 4, HEADS, BLOCK, group_rows), BF16),
        ),
        in_specs=[vm] * 17 + [sm] * 3,
        out_specs=(vm,) * 9 + (anywhere,),
        scratch_shapes=[
            v((groups, 4, BLOCK, 512), BF16),
            v((512, 3 * LANES), BF16),
            v((LANES, 512), BF16),
            v((1, 3 * LANES), F32),
            v((groups, group_rows, LANES), BF16),
            v((groups, group_rows, LANES), BF16),
            v((groups, group_rows, LANES), BF16),
            v((groups, group_rows, LANES), F32),
            v((groups, group_rows, LANES), BF16),
            v((groups, group_rows, LANES), F32),
            v((2, HEADS, BLOCK, group_rows), BF16),
            v((groups, 2, BLOCK, 512), BF16),
            v((groups, 2, BLOCK, 512), BF16),
            v((groups, BLOCK, 512), BF16),
            v((groups, BLOCK, 512), BF16),
            v((groups, 2, BLOCK, 512), F32),
            v((own, width), F32),
            v((own, 512), BF16),
            v((own, 512), BF16),
            v((own, 512), F32),
            v((own, 512), F32),
            v((ff, 512), F32),
            v((ff, 512), F32),
            v((groups, 4, BLOCK, 512), BF16),
            v((group_rows, LANES), BF16),
            v((LANES, group_rows), F32),
            v((LANES, group_rows), F32),
            v((group_rows, LANES), F32),
            v((LANES, group_rows), F32),
            v((LANES, group_rows), F32),
            v((group_rows, 3 * LANES), BF16),
            dma((2, groups, 3)),
            dma((2, groups, 3)),
            dma((2, groups, 2)),
            dma((2, groups, 2)),
            dma((2,)),
        ],
        compiler_params=pltpu.CompilerParams(
            collective_id=0, has_side_effects=True, vmem_limit_bytes=62 * 2**20
        ),
        name="layer",
    )(
        tokens, grad, wqkv, wout, upt, down, row(attn_gain), row(attn_bias), row(qkv_bias),
        row(out_bias), row(ffn_gain), row(ffn_bias), row(up_bias), row(down_bias),
        jnp.asarray(permutation(), BF16), jnp.asarray(c), jnp.asarray(s), lengths, ids, cw,
    )


def local(
    tokens, attn_norm_gain, attn_norm_bias, qkv_weight, qkv_bias, out_weight, out_bias,
    ffn_norm_gain, ffn_norm_bias, up_weight, up_bias, down_weight, down_bias, lengths,
    cluster_ids, cluster_weight, grad_out,
):
    width = tokens.shape[1]
    ff = up_bias.shape[0]
    part = jnp.stack([up_weight.T, down_weight], axis=0)
    part = lax.all_gather(part, "dp", axis=1, tiled=True)
    part = lax.all_gather(part, "heads", axis=2, tiled=True)
    part = jnp.pad(part, ((0, 0), (0, 0), (0, 512 - width)))
    result, dtok, dwqkv, dwout, dup, ddown, sums, dupb, dqkvb, _ = layer(
        tokens, qkv_weight, out_weight, part[0], part[1], attn_norm_gain, attn_norm_bias,
        qkv_bias, out_bias, ffn_norm_gain, ffn_norm_bias, up_bias, down_bias, lengths,
        cluster_ids, cluster_weight, grad_out,
    )
    dwqkv, dwout, dqkvb = lax.psum((dwqkv, dwout, dqkvb), "dp")
    sums, dupb = lax.psum((sums, dupb), ("dp", "heads"))
    grads = jnp.stack([dup[:, :width], ddown[:, :width]], axis=0)
    grads = lax.psum_scatter(grads, "heads", scatter_dimension=2, tiled=True).astype(F32)
    grads = lax.psum_scatter(grads, "dp", scatter_dimension=1, tiled=True)
    dwqkv = dwqkv.reshape(3, LANES, 512)[:, :USED, :width].reshape(3, HEADS, HD, width)
    dwqkv = dwqkv.transpose(3, 1, 0, 2).reshape(width, 3 * USED)
    dqkvb = dqkvb.reshape(3, LANES)[:, :USED].reshape(3, HEADS, HD).transpose(1, 0, 2).reshape(-1)
    return (
        result, dtok, sums[0, :width], sums[1, :width], dwqkv, dqkvb, dwout[:USED, :width],
        sums[2, :width], sums[3, :width], sums[4, :width], grads[0].T, dupb.reshape(ff),
        grads[1], sums[5, :width],
    )


def solution(mesh):
    placed = (
        P(("dp", "heads"), None), P(), P(), P(None, "heads"), P("heads"), P("heads", None), P(),
        P(), P(), P("heads", "dp"), P(), P("dp", "heads"), P(), P("dp", None), P("dp", None),
        P(), P(("dp", "heads"), None),
    )
    given = (
        P(("dp", "heads"), None), P(("dp", "heads"), None), P(), P(), P(None, "heads"), P("heads"),
        P("heads", None), P(), P(), P(), P("heads", "dp"), P(), P("dp", "heads"), P(),
    )
    return jax.shard_map(local, mesh=mesh, in_specs=placed, out_specs=given, check_vma=False)
```

time: 726 us -> 566 us (0.78)
  matrix products: 238 us -> 0 us
  local copies, waits for them, and re-layouts: 69.1 us -> 207 us
  Pallas kernels: 0 us -> 128 us
  other arithmetic: 101 us -> 5.13 us
  waiting for transfers between devices: 171 us -> 106 us
  blocking collectives: 122 us -> 93.4 us
    dot_general x48 -> x0, matrix products: 238 us -> none  [the longest x6 52 us: local(): jnp.einsum('qhd,khd->hqk', grad_block, group_values, preferred_element_ty...]
    unnamed x236 -> x34, local copies, waits for them, and re-layouts: 18.1 us -> 152 us
    pallas_call x0 -> x1, Pallas kernels: none -> 128 us  [layer(): pl.pallas_call(body, out_shape=(shape((own, width), BF16), shape((own, wi...]
    reduce_sum x17 -> x0, other arithmetic: 46.5 us -> none  [the longest x6 35.6 us: local(): denominator = jnp.sum(exp_terms, axis=-1, keepdims=True)]
    convert_element_type x6 -> x1, other arithmetic: 45.7 us -> 1.81 us  [local(): lax.psum_scatter(grads, 'heads', scatter_dimension=2, tiled=True)]
    all_gather x4 -> x1, waiting for transfers between devices: 67.8 us -> 29.1 us  [local(): part = lax.all_gather(part, 'heads', axis=2, tiled=True)]
    all_gather x2 -> x1, blocking collectives: 62.7 us -> 34.4 us  [local(): part = lax.all_gather(part, 'dp', axis=1, tiled=True)]
    slice x2 -> x4, local copies, waits for them, and re-layouts: 0.02 us -> 23.5 us  [the longest x1 21 us: local(): grads[1]]
  transfers between devices with their start and end apart: 11 -> 4, of which waited for: 7 -> 3; matrix products, arithmetic and copies ran while one was open for 35% -> 24% of each run, Pallas kernels for 0% -> 0%
where the time goes in v1:
time: 566 us; the launch traced here: 555 us
  local copies, waits for them, and re-layouts  207 us (37%)
  Pallas kernels  128 us (23%)
  waiting for transfers between devices  106 us (19%)
  blocking collectives  93.4 us (17%)
  between operations  15 us (3%)
    unnamed x34, local copies, waits for them, and re-layouts  152 us
    pallas_call x1, Pallas kernels, layer(): pl.pallas_call(body, out_shape=(shape((own, width), BF16), shape((own, wi...  128 us
    unnamed x6, waiting for transfers between devices  77.1 us
    psum x1, blocking collectives, local(): sums, dupb = lax.psum((sums, dupb), ('dp', 'heads'))  37.4 us
    all_gather x1, blocking collectives, local(): part = lax.all_gather(part, 'dp', axis=1, tiled=True)  34.4 us
    all_gather x1, waiting for transfers between devices, local(): part = lax.all_gather(part, 'heads', axis=2, tiled=True)  29.1 us
    psum x1, blocking collectives, local(): dwqkv, dwout, dqkvb = lax.psum((dwqkv, dwout, dqkvb), 'dp')  21.6 us
    slice x1, local copies, waits for them, and re-layouts, local(): grads[1]  21 us
  transfers between devices with their start and end apart: 4, of which 3 were waited for; matrix products, arithmetic and copies ran while one was open for 24% of the time, Pallas kernels for 0%

profile of v1, /device:TPU:0, one launch (start us, length us, event | category | flops | bytes accessed | tf_op | source)
XLA Modules:
  0.0 554.8 jit_solution(3711535076238687572)
XLA Ops:
  7.3 1.0 copy.81
  8.3 0.9 pad_maximum_fusion.1
  9.2 34.4 %all_gather.6 = bf16[2,1920,120]{2,1,0:T(8,128)(2,1)S(1)} all-gather(bf16[2,240,120]{2,1,0:T(8,128)(2,1)S(1)} %pad_maximum_fusion.1), channel_id=1, replica_groups=mesh['dp'=8,'heads'=4] {'dp'}, dimensions={1}, use_global_device_ids=true | all-gather | bytes 1036800 | tf_op jit(solution)/shard_map/all_gather | solution.py:589
  43.5 1.9 copy.82
  46.7 1.2 copy.84.tok
  47.9 1.2 copy.85.grad
  49.0 29.1 %all-gather.2.cloned.1.call-done = bf16[2,1920,480]{1,0,2:T(2,128)(2,1)} async-done(((bf16[2,1920,120]{1,0,2:T(2,128)(2,1)}), bf16[2,1920,480]{1,0,2:T(2,128)(2,1)}) %all-gather.2.cloned.1.call-update) | async-done | bytes 3686416 | tf_op jit(solution)/shard_map/all_gather | solution.py:590
  78.2 10.5 %copy.83 = bf16[2,1920,480]{2,1,0:T(8,128)(2,1)} copy(bf16[2,1920,480]{1,0,2:T(2,128)(2,1)} %all-gather.2.cloned.1.call-done) | data formatting | bytes 7372800 | tf_op jit(solution)/shard_map/all_gather | solution.py:590
  88.7 4.5 fusion.1
  93.2 127.7 %layer.1 = (bf16[768,480]{1,0:T(8,128)(2,1)}, f32[768,480]{1,0:T(8,128)}, f32[384,512]{1,0:T(8,128)}, f32[128,512]{1,0:T(8,128)}, bf16[1920,512]{1,0:T(8,128)(2,...) custom-call(bf16[768,480]{1,0:T(8,128)(2,1)} %copy.84.tok, ...), custom_call_target="tpu_custom_call" | custom-call | tf_op jit(solution)/shard_map/layer/pallas_call | solution.py:516
  220.9 2.4 slice_bitcast_fusion
  223.3 2.4 pad_maximum_fusion
  225.7 10.7 %copy.88 = bf16[2,1920,480]{1,0,2:T(2,128)(2,1)} copy(bf16[2,1920,480]{2,1,0:T(8,128)(2,1)} %pad_maximum_fusion) | data formatting | bytes 7372800 | tf_op jit(solution)/shard_map/stack | solution.py:599
  236.5 0.7 all-reduce.9.cloned.1.call-update
  238.5 75.5 %all-reduce.7.cloned.1.call-done = bf16[2,1920,480]{1,0,2:T(2,128)(2,1)} async-done(((bf16[2,1920,480]{1,0,2:T(2,128)(2,1)}), bf16[2,1920,480]{1,0,2:T(2,128)(2,1)}) %all-reduce.7.cloned.1.call-update) | async-done | bytes 3686416
  314.1 1.8 dynamic-slice_convert_fusion
  315.9 55.1 %copy.93 = f32[2,1920,120]{0,2,1:T(8,128)} copy(f32[2,1920,120]{1,0,2:T(2,128)S(1)} %dynamic-slice_convert_fusion) | data formatting | bytes 3686400
  371.0 62.8 %reshape.88 = f32[1920,240]{1,0:T(8,128)} reshape(f32[1920,120,2]{2,1,0:T(8,128)} %bitcast.1) | data formatting | bytes 3686400
  433.8 1.1 copy.89
  435.0 21.6 %psum.37 = f32[3,128]{1,0:T(4,128)S(1)} all-reduce(f32[3,128]{1,0:T(4,128)S(1)} %bitcast.51), channel_id=1, replica_groups=mesh['dp'=8,'heads'=4] {'dp'}, use_global_device_ids=true, to_apply=%region_2.3 | all-reduce | flops 384 | bytes 3072 | tf_op jit(solution)/shard_map/psum | solution.py:597
  456.6 0.7 reshape.86
  457.3 1.6 copy.90
  458.9 37.4 %all-reduce.2 = (f32[8,512]{1,0:T(8,128)S(1)}, f32[1920]{0:T(1024)}) all-reduce(f32[8,512]{1,0:T(8,128)S(1)} %copy-done.5, f32[1920]{0:T(1024)S(1)} %reduce.1), channel_id=1, replica_groups=mesh['dp'=8,'heads'=4] {'dp','heads'}, use_global_device_ids=true, to_apply=%region_0.1 | all-reduce | flops 6016 | bytes 48128 | tf_op jit(solution)/shard_map/psum | solution.py:598
  496.3 0.6 fusion.3
  496.9 1.2 slice.62
  498.2 1.1 copy.91
  499.3 0.7 slice.63
  500.0 0.8 reduce-scatter.4.cloned.1.call-done
  500.9 8.2 %reshape.89 = f32[240,120,2]{2,1,0:T(8,128)} reshape(f32[240,240]{1,0:T(8,128)} %reduce-scatter.4.cloned.1.call-done) | data formatting | bytes 460800
  509.0 21.0 %fusion.2 = (f32[1,240,120]{0,2,1:T(8,128)}, f32[1,240,120]{0,2,1:T(8,128)}) fusion(f32[2,240,120]{0,2,1:T(8,128)} %bitcast.41), kind=kLoop, calls=%fused_computation.9 | loop fusion | bytes 460800 | tf_op jit(solution)/shard_map/slice | solution.py:608
  530.0 8.8 %copy.95 = f32[1,240,120]{2,1,0:T(8,128)} copy(f32[1,240,120]{0,2,1:T(8,128)} %get-tuple-element.120) | data formatting | bytes 230400
  538.8 9.0 %copy.96 = f32[1,240,120]{1,2,0:T(8,128)} copy(f32[1,240,120]{0,2,1:T(8,128)} %get-tuple-element.121) | data formatting | bytes 230400
  (38 shorter events, 2.2 us)
Async XLA Ops:
  7.2 38.3 %copy-start.8 = (f32[360]{0:T(512)S(1)}, f32[360]{0:T(512)}, u32[]{:S(2)}) copy-start(f32[360]{0:T(512)} %param.24) | copy-start | bytes 4324
  7.2 38.9 %copy-start.6 = (f32[1920]{0:T(1024)S(1)}, f32[1920]{0:T(1024)}, u32[]{:S(2)}) copy-start(f32[1920]{0:T(1024)} %param.30) | copy-start | bytes 23044
  7.2 39.5 %copy-start.2 = (bf16[768,480]{0,1:T(8,128)(2,1)S(1)}, bf16[768,480]{0,1:T(8,128)(2,1)}, u32[]{:S(2)}) copy-start(bf16[768,480]{0,1:T(8,128)(2,1)} %param.20) | copy-start | bytes 2211844
  7.2 40.6 %copy-start.3 = (bf16[768,480]{0,1:T(8,128)(2,1)S(1)}, bf16[768,480]{0,1:T(8,128)(2,1)}, u32[]{:S(2)}) copy-start(bf16[768,480]{0,1:T(8,128)(2,1)} %param.36) | copy-start | bytes 2211844
  7.2 70.9 %all-gather.2.cloned.1.call-start = ((), (), s32[]{:S(2)}) async-start(), calls=%async_computation.1 | async-start | bytes 4608000 | tf_op jit(solution)/shard_map/all_gather | solution.py:590
  45.5 268.6 %all-reduce.7.cloned.1.call-start = ((), (), s32[]{:S(2)}) async-start(), calls=%async_computation.3 | async-start | bytes 7372800
  236.5 0.8 copy-start.10
  236.5 260.4 %all-reduce.9.cloned.1.call-start = ((), (), s32[]{:S(2)}) async-start(), calls=%async_computation.4 | async-start | bytes 2097152 | tf_op jit(solution)/shard_map/psum | solution.py:597
  237.2 263.6 %reduce-scatter.4.cloned.1.call-start = ((), (), s32[]{:S(2)}) async-start(), calls=%async_computation.2 | async-start | bytes 2211840
  371.0 62.8 %copy-start.1 = (bf16[768,480]{1,0:T(8,128)(2,1)S(1)}, bf16[768,480]{1,0:T(8,128)(2,1)}, u32[]{:S(2)}) copy-start(bf16[768,480]{1,0:T(8,128)(2,1)} %get-tuple-element.102) | copy-start | bytes 2211844
  371.0 63.9 %copy-start.9 = (f32[1,384]{1,0:T(1,128)S(1)}, f32[1,384]{1,0:T(1,128)}, u32[]{:S(2)}) copy-start(f32[1,384]{1,0:T(1,128)} %get-tuple-element.27) | copy-start | bytes 4612
  371.0 64.0 %copy-start.7 = (f32[1,1920]{1,0:T(1,128)S(1)}, f32[1,1920]{1,0:T(1,128)}, u32[]{:S(2)}) copy-start(f32[1,1920]{1,0:T(1,128)} %get-tuple-element.31) | copy-start | bytes 23044
  433.8 23.6 %copy-start = (f32[768,480]{1,0:T(8,128)S(1)}, f32[768,480]{1,0:T(8,128)}, u32[]{:S(2)}) copy-start(f32[768,480]{1,0:T(8,128)} %get-tuple-element.103) | copy-start | bytes 4423684
  433.8 25.1 %copy-start.5 = (f32[8,512]{1,0:T(8,128)S(1)}, f32[8,512]{1,0:T(8,128)}, u32[]{:S(2)}) copy-start(f32[8,512]{1,0:T(8,128)} %get-tuple-element.25) | copy-start | bytes 49156
  496.9 2.4 copy-start.4
Sparse Core Ops, SparseCore 0:
  45.6 32.5 all-gather.1
  236.6 77.3 all-reduce.6
  317.6 78.2 all-reduce.8
  433.9 66.8 reduce-scatter.3

commit v2 on v1

--- a/solution.py
+++ b/solution.py
@@ -18,7 +18,6 @@
 LOG2E = 1.4426950408889634
 BIG = 1e30
 BLOCK = 256
-FF_TILE = 384
 
 
 def dims(a, b, ca, cb, precision=None):
@@ -72,13 +71,13 @@
 
 
 def body(
-    tok, grad, wqkv, wout, upt, down, attn_gain, attn_bias, qkv_bias, out_bias, ffn_gain,
-    ffn_bias, up_bias, down_bias, perm, cos, sin, lengths, ids, cw,
-    result, dtok, dwqkv, dwout, dup, ddown, sums, dupb, dqkvb, phbm,
+    inner, tok, grad, wqkv, wout, w_in, attn_gain, attn_bias, qkv_bias, out_bias, ffn_gain,
+    ffn_bias, up_bias, down_bias, perm, spread, cos, sin, lengths, ids, cw,
+    result, dtok, d_first, small, phbm,
     n1, wq, wo, qkv_b, q_s, k_s, v_s, ctx, ctxb, invl, pslot,
     rs_core_out, rs_core_in, rs_y_out, rs_y_in, rs_own,
-    mid, n2, df, facc, dn2, gup, gdown, da, do_s, dot_t, q_t, dq, dk_t, dv_t, dqkv,
-    ag_s, ag_r, rs_s, rs_r, p_s,
+    mid, n2, df, n2p, dfp, facc, dn2, wup, wdown, da, do_s, dot_t, q_t, dq, dk_t, dv_t, dqkv,
+    sums, acc, ag_s, ag_r, rs_s, rs_r, p_s, remote,
 ):
     d, h = lax.axis_index("dp"), lax.axis_index("heads")
     core, y = h % 2, h // 2
@@ -125,30 +124,317 @@
         for other in (0, 1):
             rs_core_out[k, other] = part(2 * other + 1 - core).astype(BF16)
         sum_copy(use, k, 0).start()
-        for other in (0, 1):
-            rs_own[k, other] = part(2 * other + core)
+        rs_y_out[k] = part(2 * (1 - y) + core).astype(BF16)
+        rs_own[k] = part(h)
 
     def sum_forward(use, k):
         sum_copy(use, k, 0).wait_recv()
-        rs_y_out[k] = (rs_own[k, 1 - y] + rs_core_in[k, 1 - y].astype(F32)).astype(BF16)
+        rs_y_out[k] = (rs_y_out[k].astype(F32) + rs_core_in[k, 1 - y].astype(F32)).astype(BF16)
         sum_copy(use, k, 1).start()
 
     def sum_finish(use, k):
         sum_copy(use, k, 1).wait_recv()
-        return rs_own[k, y] + rs_core_in[k, y].astype(F32) + rs_y_in[k].astype(F32)
+        return rs_own[k] + rs_core_in[k, y].astype(F32) + rs_y_in[k].astype(F32)
 
     def sum_sent(use, k):
         for n in range(2):
             sum_copy(use, k, n).wait_send()
 
+    if inner:
+        (g, rc, rx, rz, ry, wsum, wall, wres, heads_in, dp_out, dp_in,
+         w_s, w_r, c_s, c_r, f_s, f_r, m_s, m_r) = remote
+        wup_in, wdown_in = w_in
+        dwqkv, dwout, dup, ddown = d_first
+        gw = gg = g
+        z, x = d // 2, d % 2
+        xpart, above, below = (d + 1 - 2 * x, h), (d + 2, h), (d - 2, h)
+        peers = [lax.rem(d + n, 8) for n in range(1, 8)]
+        greeted = [sib, ypart, (d, (h_sib + 2) % 4)] + [(p, h) for p in peers]
+    else:
+        gw, (acc_out, gg) = w_in[0], d_first
+        greeted = [sib, ypart]
+
+    def w_y():
+        block = g.at[core, z, x, y]
+        return send(block, block, w_s.at[0], w_r.at[0], ypart)
+
+    def w_up(s, origin):
+        pair = g.at[core, origin, x]
+        return send(pair, pair, w_s.at[s], w_r.at[s], above)
+
+    def w_down(s, origin):
+        pair = g.at[core, origin, x]
+        return send(pair, pair, w_s.at[3 + s], w_r.at[3 + s], below)
+
+    def w_x(origin, side):
+        pair = g.at[core, origin, side]
+        return send(pair, pair, w_s.at[7 + origin], w_r.at[7 + origin], xpart)
+
+    def w_core(origin, side, at):
+        pair = g.at[at, origin, side]
+        n = 11 + 2 * origin + side
+        return send(pair, pair, w_s.at[n], w_r.at[n], sib)
+
+    def w_begin():
+        g[core, z, x, y] = jnp.zeros((480, LANES), BF16)
+        g[core, z, x, y, 0:240, 0:USED] = wup_in[...].astype(F32).T.astype(BF16)
+        g[core, z, x, y, 240:480, 0:USED] = wdown_in[...]
+        w_y().start()
+
+    def w_here(origin):
+        w_x(origin, x).start()
+        w_core(origin, x, core).start()
+
+    def w_first():
+        w_y().wait_recv()
+
+        @pl.when(z < 3)
+        def _():
+            w_up(1, z).start()
+
+        @pl.when(z > 0)
+        def _():
+            w_down(1, z).start()
+
+        w_here(z)
+
+    def w_step(s):
+        @pl.when(z >= s)
+        def _():
+            w_up(s, z - s).wait_recv()
+            if s < 3:
+
+                @pl.when(z < 3)
+                def _():
+                    w_up(s + 1, z - s).start()
+
+            w_here(z - s)
+
+        @pl.when(z + s <= 3)
+        def _():
+            w_down(s, z + s).wait_recv()
+            if s < 3:
+
+                @pl.when(z > 0)
+                def _():
+                    w_down(s + 1, z + s).start()
+
+            w_here(z + s)
+
+    def w_other(s):
+        def one(origin):
+            w_x(origin, 1 - x).wait_recv()
+            w_core(origin, 1 - x, core).start()
+
+        if s == 0:
+            one(z)
+        else:
+            pl.when(z >= s)(lambda: one(z - s))
+            pl.when(z + s <= 3)(lambda: one(z + s))
+
+    def w_end():
+        for origin in range(4):
+            for side in (0, 1):
+                w_core(origin, side, 1 - core).wait_recv()
+
+    def w_sent():
+        w_y().wait_send()
+        for s in (1, 2, 3):
+            pl.when((z >= s - 1) & (z < 3))(lambda: w_up(s, z - s + 1).wait_send())
+            pl.when((z + s - 1 <= 3) & (z > 0))(lambda: w_down(s, z + s - 1).wait_send())
+        for origin in range(4):
+            w_x(origin, x).wait_send()
+            for side in (0, 1):
+                w_core(origin, side, core).wait_send()
+
+    def assemble():
+        def step(i, _):
+            parts = [gw[n % 2, i // 2, i % 2, n // 2] for n in range(4)]
+            full = nn(jnp.concatenate(parts, axis=1), spread[...]).astype(BF16)
+            r = pl.ds(pl.multiple_of(i * 240, 240), 240)
+            wup[r, :] = full[0:240]
+            wdown[r, :] = full[240:480]
+            return 0
+
+        lax.fori_loop(0, 8, step, 0)
+
+    order = (3, 0, 2, 1)
+
+    def g_core(origin):
+        return send(
+            g.at[1 - core, origin], rc.at[origin], c_s.at[origin], c_r.at[origin], sib
+        )
+
+    def g_x(origin):
+        return send(
+            g.at[core, origin, 1 - x], rx.at[origin], c_s.at[4 + origin], c_r.at[4 + origin], xpart
+        )
+
+    def g_up(s, to):
+        return send(g.at[core, to, x], rz.at[0, s - 1], c_s.at[7 + s], c_r.at[7 + s], above)
+
+    def g_down(s, to):
+        return send(g.at[core, to, x], rz.at[1, s - 1], c_s.at[10 + s], c_r.at[10 + s], below)
+
+    def g_y():
+        return send(g.at[core, z, x, 1 - y], ry, c_s.at[14], c_r.at[14], ypart)
+
+    def add_pair(origin, side, ref):
+        for n in (0, 1):
+            g[core, origin, side, n] = (
+                g[core, origin, side, n].astype(F32) + ref[n].astype(F32)
+            ).astype(BF16)
+
+    def g_begin():
+        for origin in order:
+            g_core(origin).start()
+
+    def g_first():
+        for origin in order:
+            g_core(origin).wait_recv()
+            add_pair(origin, 1 - x, rc.at[origin, 1 - x])
+            g_x(origin).start()
+        for origin in order:
+            add_pair(origin, x, rc.at[origin, x])
+
+    def g_add_x(origins):
+        for origin in origins:
+            g_x(origin).wait_recv()
+            add_pair(origin, x, rx.at[origin])
+
+    def g_send(s):
+        pl.when(z < s)(lambda: g_up(s, 4 - s + z).start())
+        pl.when(3 - z < s)(lambda: g_down(s, s + z - 4).start())
+
+    def g_recv(s):
+        @pl.when((z >= 1) & (z <= s))
+        def _():
+            g_up(s, 0).wait_recv()
+            add_pair(3 - s + z, x, rz.at[0, s - 1])
+
+        @pl.when((z <= 2) & (z >= 3 - s))
+        def _():
+            g_down(s, 0).wait_recv()
+            add_pair(s + z - 3, x, rz.at[1, s - 1])
+
+    def g_last():
+        g_y().wait_recv()
+        total = g[core, z, x, y].astype(F32) + ry[...].astype(F32)
+        dup[...] = total[0:240].T[0:USED]
+        ddown[...] = total[240:480, 0:USED]
+        for n in range(4):
+            g_core(n).wait_send()
+            g_x(n).wait_send()
+        for s in (1, 2, 3):
+            pl.when(z < s)(lambda: g_up(s, 0).wait_send())
+            pl.when(3 - z < s)(lambda: g_down(s, 0).wait_send())
+        g_y().wait_send()
+
+    spans = ((384, 512), (256, 384), (0, 256))
+
+    def slot_of(n):
+        first, last = spans[n]
+        size = (last - first) // 8
+        return first, size
+
+    def f_part(n, p):
+        first, size = slot_of(n)
+        return pl.ds(pl.multiple_of(first + p * size, 16), size)
+
+    def f_in(n, p):
+        first, size = slot_of(n)
+        return pl.ds(pl.multiple_of(first + p * size, 16), size)
+
+    def f_out_copy(n, p):
+        return send(
+            wall.at[f_part(n, p)], wsum.at[f_in(n, d)], f_s.at[0, n, p], f_r.at[0, n, d], (p, h)
+        )
+
+    def f_in_copy(n, p):
+        return send(
+            wall.at[f_part(n, p)], wsum.at[f_in(n, p)], f_s.at[0, n, p], f_r.at[0, n, p], (p, h)
+        )
+
+    def f_back_copy(n, p, at):
+        return send(
+            wres.at[f_part(n, at)], wres.at[f_part(n, at)], f_s.at[1, n, p], f_r.at[1, n, at], (p, h)
+        )
+
+    def f_begin(n):
+        first, last = spans[n]
+        wall[first:last, :] = acc[first:last, :].astype(BF16)
+        wsum[f_in(n, d), :] = wall[f_part(n, d), :]
+        for p in peers:
+            f_out_copy(n, p).start()
+
+    def f_back(n):
+        first, size = slot_of(n)
+        for p in peers:
+            f_in_copy(n, p).wait_recv()
+        total = jnp.zeros((size, 512), F32)
+        for p in range(8):
+            total = total + wsum[first + p * size : first + (p + 1) * size, :].astype(F32)
+        wres[f_part(n, d), :] = total.astype(BF16)
+        for p in peers:
+            f_back_copy(n, p, d).start()
+
+    def f_end(n):
+        for p in peers:
+            f_back_copy(n, p, p).wait_recv()
+
+    def f_sent(n):
+        for p in peers:
+            f_out_copy(n, p).wait_send()
+            f_back_copy(n, p, d).wait_send()
+
+    near = (sib, ypart, (d, (h_sib + 2) % 4))
+
+    def m_heads(b, n, at):
+        return send(sums.at[b], heads_in.at[b, at], m_s.at[b, n], m_r.at[b, at], near[n])
+
+    def m_dp(b, n, at):
+        return send(
+            dp_out.at[b], dp_in.at[b, at], m_s.at[b, 3 + n], m_r.at[b, 4 + at], (peers[n], h)
+        )
+
+    def m_begin(b):
+        heads_in[b, h] = sums[b]
+        for n in range(3):
+            m_heads(b, n, h).start()
+
+    def m_middle(b):
+        for n in range(3):
+            m_heads(b, n, near[n][1]).wait_recv()
+        total = heads_in[b, 0] + heads_in[b, 1] + heads_in[b, 2] + heads_in[b, 3]
+        if b == 0:
+            row = lax.broadcasted_iota(jnp.int32, total.shape, 0)
+            total = jnp.where(row == 2, sums[b], total)
+        dp_out[b] = total
+        dp_in[b, d] = total
+        for n in range(7):
+            m_dp(b, n, d).start()
+
+    def m_end(b):
+        for n in range(7):
+            m_dp(b, n, peers[n]).wait_recv()
+        total = dp_in[b, 0]
+        for p in range(1, 8):
+            total = total + dp_in[b, p]
+        small[8 * b : 8 * b + 8, :] = total
+        for n in range(3):
+            m_heads(b, n, h).wait_send()
+        for n in range(7):
+            m_dp(b, n, d).wait_send()
+
     def rows_of(k):
         return slice(k * BLOCK, (k + 1) * BLOCK)
 
     def add_sum(row, value):
-        sums[row : row + 1, 0:width] += value
+        b, at = row // 8, row % 8
+        sums[b, at : at + 1, 0 : value.shape[1]] += value
 
     barrier = pltpu.get_barrier_semaphore()
-    for other in (sib, ypart):
+    for other in greeted:
         pl.semaphore_signal(barrier, inc=1, device_id=other, device_id_type=MESH)
 
     def first_norm(k):
@@ -157,8 +443,10 @@
         n1[k, h, :, width:512] = jnp.zeros((BLOCK, 512 - width), BF16)
 
     first_norm(0)
-    pl.semaphore_wait(barrier, 2)
+    pl.semaphore_wait(barrier, len(greeted))
     gather_start(0, n1, 0)
+    if inner:
+        w_begin()
     for k in range(1, groups):
         first_norm(k)
         gather_start(0, n1, k)
@@ -171,10 +459,7 @@
         [wout[...].astype(F32), jnp.zeros((LANES - USED, width), F32)], axis=0
     ).astype(BF16)
     sums[...] = jnp.zeros_like(sums)
-    dwqkv[...] = jnp.zeros_like(dwqkv)
-    dwout[...] = jnp.zeros_like(dwout)
-    dqkvb[...] = jnp.zeros_like(dqkvb)
-    dupb[...] = jnp.zeros_like(dupb)
+    acc[...] = jnp.zeros_like(acc)
     n2[:, width:512] = jnp.zeros((groups * BLOCK, 512 - width), BF16)
     df[:, width:512] = jnp.zeros((groups * BLOCK, 512 - width), BF16)
     for k in range(groups):
@@ -198,22 +483,22 @@
 
         def step(i, _):
             r = pl.ds(pl.multiple_of(i * BLOCK, BLOCK), BLOCK)
-            x = nn(n1[k, i], wq[...]) + qkv_b[...]
+            x_ = nn(n1[k, i], wq[...]) + qkv_b[...]
             c, s = cos[r, :], sin[r, :]
             at = lane(BLOCK)
             row = lax.broadcasted_iota(jnp.int32, (BLOCK, LANES), 0) + i * BLOCK
             inside = (row >= lo) & (row < hi)
             marks = (at >= USED) & (at < USED + 5)
-            q = x[:, 0:LANES]
+            q = x_[:, 0:LANES]
             q = (q * c + partner(q) * s) * (HD ** (-0.5) * LOG2E)
             q_s[k, r, :] = jnp.where(at < USED, q, jnp.where(inside, 1.0, 0.0)).astype(BF16)
-            key = x[:, LANES : 2 * LANES]
+            key = x_[:, LANES : 2 * LANES]
             key = key * c + partner(key) * s
             k_s[k, r, :] = jnp.where(
                 at < USED, key, jnp.where(marks & jnp.logical_not(inside), -BIG, 0.0)
             ).astype(BF16)
             v_s[k, r, :] = jnp.where(
-                at < USED, x[:, 2 * LANES : 3 * LANES], jnp.where(at < USED + 2, 1.0, 0.0)
+                at < USED, x_[:, 2 * LANES : 3 * LANES], jnp.where(at < USED + 2, 1.0, 0.0)
             ).astype(BF16)
             return 0
 
@@ -227,10 +512,19 @@
         slot = n % 2
         return pltpu.make_async_copy(phbm.at[n // steps, n % steps], pslot.at[slot], p_s.at[slot])
 
-    def attend(k, first, last):
+    def run_hooks(hooks, i):
+        for at, todo in hooks.items():
+
+            @pl.when(i == at)
+            def _():
+                for one in todo:
+                    one()
+
+    def attend(k, hooks):
         def step(i, _):
             n = k * steps + i
             slot = n % 2
+            run_hooks(hooks, i)
 
             @pl.when(n >= 2)
             def _():
@@ -244,7 +538,7 @@
             def score(j):
                 return nt(jnp.where(head_lanes(BLOCK, j) | (at >= USED), q, 0), keys)
 
-            acc = jnp.zeros((BLOCK, LANES), F32)
+            out = jnp.zeros((BLOCK, LANES), F32)
             inv = jnp.zeros((BLOCK, LANES), F32)
             s = score(0)
             for j in range(HEADS):
@@ -253,16 +547,16 @@
                 pslot[slot, j] = e
                 o = nn(e, vals)
                 one = 1.0 / o[:, USED : USED + 1]
-                acc = jnp.where(head_lanes(BLOCK, j), o * one, acc)
+                out = jnp.where(head_lanes(BLOCK, j), o * one, out)
                 inv = jnp.where(head_lanes(BLOCK, j), one, inv)
                 s = later
-            ctx[k, r, :] = acc
-            ctxb[k, r, :] = acc.astype(BF16)
+            ctx[k, r, :] = out
+            ctxb[k, r, :] = out.astype(BF16)
             invl[k, r, :] = inv
             p_out(k, i).start()
             return 0
 
-        lax.fori_loop(first, last, step, 0)
+        lax.fori_loop(0, steps, step, 0)
 
     def out_part(k):
         def part(i):
@@ -277,16 +571,30 @@
         project(k)
         if k > 0:
             sum_forward(0, k - 1)
-        attend(k, 0, steps - 1)
+        hooks = {}
         if k + 1 < groups:
-            gather_forward(0, n1, k + 1)
-        attend(k, steps - 1, steps)
+            hooks[3] = [partial(gather_forward, 0, n1, k + 1)]
+        if inner:
+            if k == 0:
+                hooks[0] = [w_first]
+                hooks[3] += [partial(w_step, 1), partial(w_other, 0)]
+            if k == 1:
+                hooks[2] = [partial(w_step, 2), partial(w_other, 1)]
+            if k == 2:
+                hooks[0] = [partial(w_step, 3), partial(w_other, 2)]
+                hooks[3] = [partial(w_other, 3)]
+        attend(k, hooks)
         sum_start(0, k, out_part(k))
     sum_forward(0, groups - 1)
     for n in (groups * steps, groups * steps + 1):
         p_in(n % 2).wait()
     p_in(0).start()
     p_in(1).start()
+    if inner:
+        w_end()
+    assemble()
+    if inner:
+        w_sent()
 
     def weight_of(k):
         ends = ends_of(k)
@@ -304,24 +612,24 @@
         n2[r, 0:width] = (xhat * ffn_gain[...] + ffn_bias[...]).astype(BF16)
         d_ffn = (grad[r, :].astype(F32) * weight_of(k)).astype(BF16)
         df[r, 0:width] = d_ffn
-        add_sum(5, jnp.sum(d_ffn.astype(F32), axis=0, keepdims=True))
+        add_sum(15, jnp.sum(d_ffn.astype(F32), axis=0, keepdims=True))
+        n2p[r, :] = nt(n2[r, :], spread[...]).astype(BF16)
+        dfp[r, :] = nt(df[r, :], spread[...]).astype(BF16)
 
     def ffn_core(first, last):
         r = slice(first * BLOCK, last * BLOCK)
 
         def step(t, _):
-            f = pl.ds(pl.multiple_of(t * FF_TILE, FF_TILE), FF_TILE)
-            wu, wd = upt[f, :], down[f, :]
-            x, g = n2[r, :], df[r, :]
-            u = nt(x, wu) + up_bias[:, f]
+            f = pl.ds(pl.multiple_of(t * 480, 480), 480)
+            wu, wd = wup[f, :], wdown[f, :]
+            u = nt(n2[r, :], wu) + up_bias[pl.ds(t, 1), :]
             phi = 0.5 + 0.5 * lax.erf(u * (0.5**0.5))
             hid = (u * phi).astype(BF16)
             slope = phi + u * (jnp.exp(u * u * -0.5) * 0.3989422804014327)
             out = nn(hid, wd)
-            du = (nt(g, wd) * slope).astype(BF16)
+            du = (nt(df[r, :], wd) * slope).astype(BF16)
             dx = nn(du, wu)
-            gu, gd = tn(du, x), tn(hid, g)
-            dupb[:, f] += jnp.sum(du.astype(F32), axis=0, keepdims=True)
+            sums[1, pl.ds(t, 1), 0:480] += jnp.sum(du.astype(F32), axis=0, keepdims=True)
 
             @pl.when(t == 0)
             def _():
@@ -333,30 +641,32 @@
                 facc[r, :] += out
                 dn2[r, :] += dx
 
-            if first == 0:
-                gup[f, :] = gu
-                gdown[f, :] = gd
-            else:
-                gup[f, :] += gu
-                gdown[f, :] += gd
+            for part, wide in enumerate((tn(du, n2p[r, :]), tn(hid, dfp[r, :]))):
+                fr = slice(part * 240, part * 240 + 240)
+                for side in (0, 1):
+                    for n in range(4):
+                        new = wide[side * 240 : side * 240 + 240, n * LANES : (n + 1) * LANES]
+                        if first > 0:
+                            new = new + gg[n % 2, t, side, n // 2, fr, :].astype(F32)
+                        gg[n % 2, t, side, n // 2, fr, :] = new.astype(BF16)
             return 0
 
-        lax.fori_loop(0, upt.shape[0] // FF_TILE, step, 0)
+        lax.fori_loop(0, 4, step, 0)
 
     def ffn_post(k):
         r = rows_of(k)
         middle = mid[r, :]
         result[r, :] = (middle + facc[r, 0:width] + down_bias[...]).astype(BF16)
-        g = dn2[r, 0:width]
+        g_ = dn2[r, 0:width]
         xhat, rstd = norm(middle)
-        add_sum(3, jnp.sum(g * xhat, axis=0, keepdims=True))
-        add_sum(4, jnp.sum(g, axis=0, keepdims=True))
+        add_sum(13, jnp.sum(g_ * xhat, axis=0, keepdims=True))
+        add_sum(14, jnp.sum(g_, axis=0, keepdims=True))
         d_result = grad[r, :].astype(F32) * weight_of(k)
-        d_middle = d_result + norm_back(g, ffn_gain[...], xhat, rstd)
+        d_middle = d_result + norm_back(g_, ffn_gain[...], xhat, rstd)
         dtok[r, :] = d_middle
         low = d_middle.astype(BF16)
         da[k, h, :, 0:width] = low
-        add_sum(2, jnp.sum(low.astype(F32), axis=0, keepdims=True))
+        add_sum(12, jnp.sum(low.astype(F32), axis=0, keepdims=True))
         gather_start(1, da, k)
 
     for k in range(groups - 1):
@@ -366,9 +676,11 @@
         ffn_post(k)
     ffn_pre(groups - 1)
     ffn_core(groups - 1, groups)
+    if inner:
+        g_begin()
     ffn_post(groups - 1)
-    dup[...] = gup[...].astype(BF16)
-    ddown[...] = gdown[...].astype(BF16)
+    if inner:
+        m_begin(1)
     for k in range(groups):
         gather_sent(0, n1, k)
         sum_sent(0, k)
@@ -376,48 +688,49 @@
     def back_prep(k):
         def step(i, _):
             r = pl.ds(pl.multiple_of(i * BLOCK, BLOCK), BLOCK)
-            g = nt(da[k, i], wo[...]).astype(BF16).astype(F32)
-            g = (g * invl[k, r, :]).astype(BF16)
-            do_s[r, :] = g
-            dot_t[:, r] = g.astype(F32).T
+            g_ = nt(da[k, i], wo[...]).astype(BF16).astype(F32)
+            g_ = (g_ * invl[k, r, :]).astype(BF16)
+            do_s[r, :] = g_
+            dot_t[:, r] = g_.astype(F32).T
             q_t[:, r] = q_s[k, r, :].astype(F32).T
-            dwout[...] += tn(ctxb[k, r, :], da[k, i])
+            acc[3 * LANES : 4 * LANES, :] += tn(ctxb[k, r, :], da[k, i])
             return 0
 
         lax.fori_loop(0, steps, step, 0)
         dk_t[...] = jnp.zeros_like(dk_t)
         dv_t[...] = jnp.zeros_like(dv_t)
 
-    def back(k, first, last):
+    def back(k, hooks):
         def step(i, _):
             n = k * steps + i
             slot = n % 2
+            run_hooks(hooks, i)
             p_in(n).wait()
             r = pl.ds(pl.multiple_of(i * BLOCK, BLOCK), BLOCK)
-            g = do_s[r, :].astype(F32)
-            prod = g * ctx[k, r, :]
+            g_ = do_s[r, :].astype(F32)
+            prod = g_ * ctx[k, r, :]
             keys, vals = k_s[k], v_s[k]
             at = lane(BLOCK)
 
             def d_prob(j):
                 mine = head_lanes(BLOCK, j)
-                inner = jnp.sum(jnp.where(mine, prod, 0.0), axis=1, keepdims=True)
-                top = inner.astype(BF16).astype(F32)
-                row = jnp.where(at == USED, -top, jnp.where(at == USED + 1, top - inner, 0.0))
-                return nt(jnp.where(mine, g, row).astype(BF16), vals)
-
-            acc = jnp.zeros((BLOCK, LANES), F32)
+                total = jnp.sum(jnp.where(mine, prod, 0.0), axis=1, keepdims=True)
+                top = total.astype(BF16).astype(F32)
+                row = jnp.where(at == USED, -top, jnp.where(at == USED + 1, top - total, 0.0))
+                return nt(jnp.where(mine, g_, row).astype(BF16), vals)
+
+            out = jnp.zeros((BLOCK, LANES), F32)
             dp = d_prob(0)
             for j in range(HEADS):
                 later = d_prob(j + 1) if j + 1 < HEADS else None
                 e = pslot[slot, j]
                 ds = (e.astype(F32) * dp).astype(BF16)
-                acc = jnp.where(head_lanes(BLOCK, j), nn(ds, keys), acc)
+                out = jnp.where(head_lanes(BLOCK, j), nn(ds, keys), out)
                 hs = slice(j * HD, (j + 1) * HD)
                 dk_t[hs, :] += nn(q_t[hs, r].astype(BF16), ds)
                 dv_t[hs, :] += nn(dot_t[hs, r].astype(BF16), e)
                 dp = later
-            dq[r, :] = acc
+            dq[r, :] = out
 
             @pl.when(n + 2 < groups * steps)
             def _():
@@ -425,7 +738,7 @@
 
             return 0
 
-        lax.fori_loop(first, last, step, 0)
+        lax.fori_loop(0, steps, step, 0)
 
     def back_post(k):
         def step(i, _):
@@ -435,10 +748,10 @@
             a = a * c - partner(a) * s
             b = dk_t[:, r].T * (1.0 / LOG2E)
             b = b * c - partner(b) * s
-            g = jnp.concatenate([a, b, dv_t[:, r].T], axis=1).astype(BF16)
-            dqkv[r, :] = g
-            dqkvb[...] += jnp.sum(g.astype(F32), axis=0, keepdims=True)
-            dwqkv[...] += tn(g, n1[k, i])
+            g_ = jnp.concatenate([a, b, dv_t[:, r].T], axis=1).astype(BF16)
+            dqkv[r, :] = g_
+            add_sum(2, jnp.sum(g_.astype(F32), axis=0, keepdims=True))
+            acc[0 : 3 * LANES, :] += tn(g_, n1[k, i])
             return 0
 
         lax.fori_loop(0, steps, step, 0)
@@ -449,11 +762,11 @@
 
     def last_norm(k):
         r = rows_of(k)
-        g = sum_finish(1, k)[:, 0:width]
+        g_ = sum_finish(1, k)[:, 0:width]
         xhat, rstd = norm(tok[r, :].astype(F32))
-        add_sum(0, jnp.sum(g * xhat, axis=0, keepdims=True))
-        add_sum(1, jnp.sum(g, axis=0, keepdims=True))
-        dtok[r, :] += norm_back(g, attn_gain[...], xhat, rstd)
+        add_sum(0, jnp.sum(g_ * xhat, axis=0, keepdims=True))
+        add_sum(1, jnp.sum(g_, axis=0, keepdims=True))
+        dtok[r, :] += norm_back(g_, attn_gain[...], xhat, rstd)
 
     for k in range(groups - 1):
         gather_forward(1, da, k)
@@ -462,18 +775,48 @@
         back_prep(k)
         if k > 0:
             sum_forward(1, k - 1)
+        hooks = {}
         if k == 0:
-            back(k, 0, 1)
-            gather_forward(1, da, groups - 1)
-            back(k, 1, steps)
-        else:
-            back(k, 0, steps)
+            hooks[1] = [partial(gather_forward, 1, da, groups - 1)]
+        if inner:
+            if k == 0:
+                hooks[0] = [g_first, partial(m_middle, 1)]
+            if k == 1:
+                hooks[0] = [partial(g_add_x, order[:2]), partial(g_send, 1), partial(m_end, 1)]
+                hooks[3] = [partial(g_add_x, order[2:]), partial(g_recv, 1), partial(g_send, 2)]
+            if k == 2:
+                hooks[0] = [partial(f_begin, 0)]
+                hooks[1] = [partial(g_recv, 2), partial(g_send, 3)]
+                hooks[2] = [partial(f_back, 0)]
+                hooks[3] = [partial(g_recv, 3), g_y().start]
+        back(k, hooks)
         back_post(k)
+        if inner and k == groups - 1:
+            f_begin(1)
+            f_begin(2)
         sum_start(1, k, tokens_part)
     for k in range(groups - 1):
         last_norm(k)
     sum_forward(1, groups - 1)
+    if inner:
+        f_back(1)
+        f_back(2)
     last_norm(groups - 1)
+    if inner:
+        m_begin(0)
+        g_last()
+        m_middle(0)
+        for n in range(3):
+            f_end(n)
+        dwqkv[...] = dims(wres[0 : 3 * LANES, :], perm[...], 0, 1)[0:width]
+        dwout[...] = wres[3 * LANES : 4 * LANES, :].astype(F32)[0:USED, 0:width]
+        m_end(0)
+        for n in range(3):
+            f_sent(n)
+    else:
+        small[0:8, :] = sums[0]
+        small[8:16, :] = sums[1]
+        acc_out[...] = acc[...]
     for k in range(groups):
         gather_sent(1, da, k)
         sum_sent(1, k)
@@ -498,8 +841,16 @@
     return c, s
 
 
+def spreading():
+    table = np.zeros((4 * LANES, 4 * LANES), np.float32)
+    for n in range(4):
+        for i in range(USED):
+            table[n * LANES + i, n * USED + i] = 1.0
+    return table
+
+
 def layer(
-    tokens, wqkv, wout, upt, down, attn_gain, attn_bias, qkv_bias, out_bias, ffn_gain,
+    inner, tokens, wqkv, wout, w_in, attn_gain, attn_bias, qkv_bias, out_bias, ffn_gain,
     ffn_bias, up_bias, down_bias, lengths, ids, cw, grad,
 ):
     own, width = tokens.shape
@@ -513,22 +864,49 @@
     shape = jax.ShapeDtypeStruct
     row = lambda v: v.reshape(1, -1)
     v, dma = pltpu.VMEM, pltpu.SemaphoreType.DMA
+    chunks = (2, 4, 2, 2, 480, LANES)
+    if inner:
+        first = (
+            shape((width, 3 * USED), F32),
+            shape((USED, width), F32),
+            shape((USED, 240), F32),
+            shape((240, USED), F32),
+        )
+        remote = [
+            v(chunks, BF16),
+            v((4, 2, 2, 480, LANES), BF16),
+            v((4, 2, 480, LANES), BF16),
+            v((2, 3, 2, 480, LANES), BF16),
+            v((480, LANES), BF16),
+            v((4 * LANES, 512), BF16),
+            v((4 * LANES, 512), BF16),
+            v((4 * LANES, 512), BF16),
+            v((2, 4, 8, 512), F32),
+            v((2, 8, 512), F32),
+            v((2, 8, 8, 512), F32),
+            dma((19,)),
+            dma((19,)),
+            dma((15,)),
+            dma((15,)),
+            dma((2, 3, 8)),
+            dma((2, 3, 8)),
+            dma((2, 10)),
+            dma((2, 12)),
+        ]
+    else:
+        first = (shape((4 * LANES, 512), F32), shape(chunks, BF16))
+        remote = []
     return pl.pallas_call(
-        body,
+        partial(body, inner),
         out_shape=(
             shape((own, width), BF16),
             shape((own, width), F32),
-            shape((3 * LANES, 512), F32),
-            shape((LANES, 512), F32),
-            shape((ff, 512), BF16),
-            shape((ff, 512), BF16),
-            shape((8, 512), F32),
-            shape((1, ff), F32),
-            shape((1, 3 * LANES), F32),
+            first,
+            shape((16, 512), F32),
             shape((groups, 4, HEADS, BLOCK, group_rows), BF16),
         ),
-        in_specs=[vm] * 17 + [sm] * 3,
-        out_specs=(vm,) * 9 + (anywhere,),
+        in_specs=[vm] * 4 + [[vm] * len(w_in)] + [vm] * 12 + [sm] * 3,
+        out_specs=(vm, vm, (vm,) * len(first), vm, anywhere),
         scratch_shapes=[
             v((groups, 4, BLOCK, 512), BF16),
             v((512, 3 * LANES), BF16),
@@ -545,14 +923,16 @@
             v((groups, 2, BLOCK, 512), BF16),
             v((groups, BLOCK, 512), BF16),
             v((groups, BLOCK, 512), BF16),
-            v((groups, 2, BLOCK, 512), F32),
+            v((groups, BLOCK, 512), F32),
             v((own, width), F32),
+            v((own, 512), BF16),
+            v((own, 512), BF16),
             v((own, 512), BF16),
             v((own, 512), BF16),
             v((own, 512), F32),
             v((own, 512), F32),
-            v((ff, 512), F32),
-            v((ff, 512), F32),
+            v((ff, 512), BF16),
+            v((ff, 512), BF16),
             v((groups, 4, BLOCK, 512), BF16),
             v((group_rows, LANES), BF16),
             v((LANES, group_rows), F32),
@@ -561,20 +941,24 @@
             v((LANES, group_rows), F32),
             v((LANES, group_rows), F32),
             v((group_rows, 3 * LANES), BF16),
+            v((2, 8, 512), F32),
+            v((4 * LANES, 512), F32),
             dma((2, groups, 3)),
             dma((2, groups, 3)),
             dma((2, groups, 2)),
             dma((2, groups, 2)),
             dma((2,)),
+            remote,
         ],
         compiler_params=pltpu.CompilerParams(
             collective_id=0, has_side_effects=True, vmem_limit_bytes=62 * 2**20
         ),
         name="layer",
     )(
-        tokens, grad, wqkv, wout, upt, down, row(attn_gain), row(attn_bias), row(qkv_bias),
-        row(out_bias), row(ffn_gain), row(ffn_bias), row(up_bias), row(down_bias),
-        jnp.asarray(permutation(), BF16), jnp.asarray(c), jnp.asarray(s), lengths, ids, cw,
+        tokens, grad, wqkv, wout, w_in, row(attn_gain), row(attn_bias), row(qkv_bias),
+        row(out_bias), row(ffn_gain), row(ffn_bias), up_bias.reshape(4, 480), row(down_bias),
+        jnp.asarray(permutation(), BF16), jnp.asarray(spreading(), BF16), jnp.asarray(c),
+        jnp.asarray(s), lengths, ids, cw,
     )
 
 
@@ -585,27 +969,41 @@
 ):
     width = tokens.shape[1]
     ff = up_bias.shape[0]
-    part = jnp.stack([up_weight.T, down_weight], axis=0)
-    part = lax.all_gather(part, "dp", axis=1, tiled=True)
-    part = lax.all_gather(part, "heads", axis=2, tiled=True)
-    part = jnp.pad(part, ((0, 0), (0, 0), (0, 512 - width)))
-    result, dtok, dwqkv, dwout, dup, ddown, sums, dupb, dqkvb, _ = layer(
-        tokens, qkv_weight, out_weight, part[0], part[1], attn_norm_gain, attn_norm_bias,
+    inner = lax.axis_size("dp") == 8
+    if inner:
+        w_in = [up_weight, down_weight]
+    else:
+        part = jnp.stack([up_weight.T, down_weight], axis=0)
+        part = lax.all_gather(part, "dp", axis=1, tiled=True)
+        part = lax.all_gather(part, "heads", axis=0)
+        part = jnp.pad(part, ((0, 0),) * 3 + ((0, LANES - USED),))
+        part = part.reshape(2, 2, 2, 4, 2, 240, LANES)
+        w_in = [part.transpose(1, 3, 4, 0, 2, 5, 6).reshape(2, 4, 2, 2, 480, LANES)]
+    result, dtok, first, small, _ = layer(
+        inner, tokens, qkv_weight, out_weight, w_in, attn_norm_gain, attn_norm_bias,
         qkv_bias, out_bias, ffn_norm_gain, ffn_norm_bias, up_bias, down_bias, lengths,
         cluster_ids, cluster_weight, grad_out,
     )
-    dwqkv, dwout, dqkvb = lax.psum((dwqkv, dwout, dqkvb), "dp")
-    sums, dupb = lax.psum((sums, dupb), ("dp", "heads"))
-    grads = jnp.stack([dup[:, :width], ddown[:, :width]], axis=0)
-    grads = lax.psum_scatter(grads, "heads", scatter_dimension=2, tiled=True).astype(F32)
-    grads = lax.psum_scatter(grads, "dp", scatter_dimension=1, tiled=True)
-    dwqkv = dwqkv.reshape(3, LANES, 512)[:, :USED, :width].reshape(3, HEADS, HD, width)
-    dwqkv = dwqkv.transpose(3, 1, 0, 2).reshape(width, 3 * USED)
-    dqkvb = dqkvb.reshape(3, LANES)[:, :USED].reshape(3, HEADS, HD).transpose(1, 0, 2).reshape(-1)
+    if inner:
+        dwqkv, dwout, dup, ddown = first
+    else:
+        acc, grads = first
+        acc, own_sums = lax.psum((acc, small[2]), "dp")
+        small = lax.psum(small, ("dp", "heads")).at[2].set(own_sums)
+        grads = grads.reshape(2, 4, 2, 2, 2, 240, LANES).transpose(3, 0, 4, 1, 2, 5, 6)
+        grads = grads.reshape(4, 2, ff, LANES)[..., :USED]
+        grads = lax.psum_scatter(grads, "heads", scatter_dimension=0).astype(F32)
+        grads = lax.psum_scatter(grads, "dp", scatter_dimension=1, tiled=True)
+        dup, ddown = grads[0].T, grads[1]
+        dwqkv = acc[: 3 * LANES, :width].reshape(3, LANES, width)[:, :USED]
+        dwqkv = dwqkv.reshape(3, HEADS, HD, width).transpose(3, 1, 0, 2).reshape(width, 3 * USED)
+        dwout = acc[3 * LANES : 3 * LANES + USED, :width]
+    dqkvb = small[2, : 3 * LANES].reshape(3, LANES)[:, :USED].reshape(3, HEADS, HD)
+    dqkvb = dqkvb.transpose(1, 0, 2).reshape(-1)
     return (
-        result, dtok, sums[0, :width], sums[1, :width], dwqkv, dqkvb, dwout[:USED, :width],
-        sums[2, :width], sums[3, :width], sums[4, :width], grads[0].T, dupb.reshape(ff),
-        grads[1], sums[5, :width],
+        result, dtok, small[0, :width], small[1, :width], dwqkv, dqkvb, dwout,
+        small[12, :width], small[13, :width], small[14, :width], dup,
+        small[8:12, :480].reshape(ff), ddown, small[15, :width],
     )
 
 

time: 566 us -> 187 us (0.33); the launches traced: 555 us -> 186 us
  local copies, waits for them, and re-layouts: 207 us -> 17.3 us
  waiting for transfers between devices: 106 us -> 0 us
  blocking collectives: 93.4 us -> 0 us
  Pallas kernels: 128 us -> 168 us
  between operations: 15 us -> 0.68 us
    unnamed x34 -> x20, local copies, waits for them, and re-layouts: 152 us -> 10.3 us
    unnamed x6 -> x0, waiting for transfers between devices: 77.1 us -> none
    psum x2 -> x0, blocking collectives: 59 us -> none  [the longest x1 37.4 us: local(): sums, dupb = lax.psum((sums, dupb), ('dp', 'heads'))]
    pallas_call x1, Pallas kernels: 128 us -> 168 us  [layer(): pl.pallas_call(partial(body, inner), out_shape=(shape((own, width), BF16)...]
    all_gather x1 -> x0, blocking collectives: 34.4 us -> none  [local(): part = lax.all_gather(part, 'dp', axis=1, tiled=True)]
    all_gather x1 -> x0, waiting for transfers between devices: 29.1 us -> none  [local(): part = lax.all_gather(part, 'heads', axis=2, tiled=True)]
    slice x4 -> x3, local copies, waits for them, and re-layouts: 23.5 us -> 2.91 us  [the longest x1 1.47 us: local(): small[15, :width]]
    another operation x2 -> x0, local copies, waits for them, and re-layouts: 13.1 us -> none  [local(): grads = jnp.stack([dup[:, :width], ddown[:, :width]], axis=0)]
  transfers between devices with their start and end apart: 4 -> 0, of which waited for: 3 -> 0; matrix products, arithmetic and copies ran while one was open for 24% -> 0% of each run, Pallas kernels for 0% -> 0%
where the time goes in v2:
time: 187 us; the launch traced here: 186 us
  Pallas kernels  168 us (90%)
  local copies, waits for them, and re-layouts  17.3 us (9%)
    pallas_call x1, Pallas kernels, layer(): pl.pallas_call(partial(body, inner), out_shape=(shape((own, width), BF16)...  168 us
    unnamed x20, local copies, waits for them, and re-layouts  10.3 us

profile of v2, /device:TPU:0, one launch (start us, length us, event | category | flops | bytes accessed | tf_op | source)
XLA Modules:
  0.0 186.3 jit_solution(17543432868965210839)
XLA Ops:
  0.6 0.0 copy-start.1
  0.7 1.3 reshape.63.qkv_bias
  2.0 1.4 reshape.67.up_bias
  3.3 2.3 %copy.39.tok = bf16[768,480]{1,0:T(8,128)(2,1)} copy(bf16[768,480]{0,1:T(8,128)(2,1)} %param.21) | data formatting | bytes 1474560 | tf_op args[0]
  5.6 0.0 copy-done.1
  5.6 1.2 copy.40.grad
  6.8 168.3 %layer.1 = (bf16[768,480]{1,0:T(8,128)(2,1)}, f32[768,480]{1,0:T(8,128)}, f32[480,360]{1,0:T(8,128)}, f32[120,480]{1,0:T(8,128)}, f32[120,240]{1,0:T(8,128)}, /*...) custom-call(bf16[768,480]{1,0:T(8,128)(2,1)} %copy.39.tok, ...), custom_call_target="tpu_custom_call" | custom-call | tf_op jit(solution)/shard_map/layer/pallas_call | solution.py:899
  175.1 0.0 copy-start
  175.1 2.4 %copy.42 = bf16[768,480]{0,1:T(8,128)(2,1)} copy(bf16[768,480]{1,0:T(8,128)(2,1)} %get-tuple-element.42) | data formatting | bytes 1474560
  177.5 0.7 slice_reduce_fusion
  178.2 0.7 slice.34
  178.9 1.5 fusion
  180.4 0.0 copy-start.2
  180.4 0.7 reshape.71
  181.1 0.1 reshape.69
  181.2 0.7 reshape.70
  181.9 0.0 copy-done
  181.9 0.0 copy-start.3
  181.9 1.6 copy.43
  183.4 0.0 copy-done.2
  183.4 0.0 copy-start.5
  183.4 0.0 copy-start.4
  183.4 0.9 copy.48
  184.3 0.0 copy-done.3
  184.3 0.7 copy.49
  185.0 0.0 copy-done.5
  185.0 0.6 copy.50
  185.7 0.0 copy-done.4
  185.7 0.6 copy.51
  (1 shorter events, 0.0 us)
Async XLA Ops:
  0.6 5.0 %copy-start.1 = (bf16[768,480]{0,1:T(8,128)(2,1)S(1)}, bf16[768,480]{0,1:T(8,128)(2,1)}, u32[]{:S(2)}) copy-start(bf16[768,480]{0,1:T(8,128)(2,1)} %param.37) | copy-start | bytes 2211844
  175.1 6.7 %copy-start = (f32[768,480]{1,0:T(8,128)S(1)}, f32[768,480]{1,0:T(8,128)}, u32[]{:S(2)}) copy-start(f32[768,480]{1,0:T(8,128)} %get-tuple-element.43) | copy-start | bytes 4423684
  180.4 3.0 %copy-start.2 = (f32[480,360]{1,0:T(8,128)S(1)}, f32[480,360]{1,0:T(8,128)}, u32[]{:S(2)}) copy-start(f32[480,360]{1,0:T(8,128)} %get-tuple-element.80) | copy-start | bytes 2073604
  181.9 2.4 %copy-start.3 = (f32[120,480]{1,0:T(8,128)S(1)}, f32[120,480]{1,0:T(8,128)}, u32[]{:S(2)}) copy-start(f32[120,480]{1,0:T(8,128)} %get-tuple-element.82) | copy-start | bytes 691204
  183.4 1.6 copy-start.5
  183.4 2.2 %copy-start.4 = (f32[240,120]{1,0:T(8,128)S(1)}, f32[240,120]{1,0:T(8,128)}, u32[]{:S(2)}) copy-start(f32[240,120]{1,0:T(8,128)} %get-tuple-element.88) | copy-start | bytes 345604

commit v3 on v2

--- a/solution.py
+++ b/solution.py
@@ -71,10 +71,11 @@
 
 
 def body(
-    inner, tok, grad, wqkv, wout, w_in, attn_gain, attn_bias, qkv_bias, out_bias, ffn_gain,
+    inner, tok_hbm, grad_hbm, wqkv, wout, w_in, attn_gain, attn_bias, qkv_bias, out_bias, ffn_gain,
     ffn_bias, up_bias, down_bias, perm, spread, cos, sin, lengths, ids, cw,
-    result, dtok, d_first, small, phbm,
-    n1, wq, wo, qkv_b, q_s, k_s, v_s, ctx, ctxb, invl, pslot,
+    result, dtok_out, d_first, small, phbm,
+    grad_t, tok, grad, in_s,
+    n1, wq, wqt, wo, qkv_b, q_s, k_s, v_s, ctx, invl, pslot,
     rs_core_out, rs_core_in, rs_y_out, rs_y_in, rs_own,
     mid, n2, df, n2p, dfp, facc, dn2, wup, wdown, da, do_s, dot_t, q_t, dq, dk_t, dv_t, dqkv,
     sums, acc, ag_s, ag_r, rs_s, rs_r, p_s, remote,
@@ -141,7 +142,7 @@
             sum_copy(use, k, n).wait_send()
 
     if inner:
-        (g, rc, rx, rz, ry, wsum, wall, wres, heads_in, dp_out, dp_in,
+        (g, rc, rx, rz, ry, f_send, f_got, wres, vecs, heads_in, dp_out, dp_in,
          w_s, w_r, c_s, c_r, f_s, f_r, m_s, m_r) = remote
         wup_in, wdown_in = w_in
         dwqkv, dwout, dup, ddown = d_first
@@ -155,76 +156,66 @@
         greeted = [sib, ypart]
 
     def w_y():
-        block = g.at[core, z, x, y]
+        block = g.at[core, y, z, x]
         return send(block, block, w_s.at[0], w_r.at[0], ypart)
 
-    def w_up(s, origin):
-        pair = g.at[core, origin, x]
-        return send(pair, pair, w_s.at[s], w_r.at[s], above)
-
-    def w_down(s, origin):
-        pair = g.at[core, origin, x]
-        return send(pair, pair, w_s.at[3 + s], w_r.at[3 + s], below)
-
-    def w_x(origin, side):
-        pair = g.at[core, origin, side]
-        return send(pair, pair, w_s.at[7 + origin], w_r.at[7 + origin], xpart)
-
-    def w_core(origin, side, at):
-        pair = g.at[at, origin, side]
-        n = 11 + 2 * origin + side
-        return send(pair, pair, w_s.at[n], w_r.at[n], sib)
+    def w_up(v, s, origin):
+        block = g.at[core, y + v - 2 * y * v, origin, x]
+        n = 3 * v + s
+        return send(block, block, w_s.at[n], w_r.at[n], above)
+
+    def w_down(v, s, origin):
+        block = g.at[core, y + v - 2 * y * v, origin, x]
+        n = 6 + 3 * v + s
+        return send(block, block, w_s.at[n], w_r.at[n], below)
+
+    def w_x(v, origin, side):
+        block = g.at[core, y + v - 2 * y * v, origin, side]
+        n = 13 + 4 * v + origin
+        return send(block, block, w_s.at[n], w_r.at[n], xpart)
+
+    def w_core(v, origin, side, at):
+        block = g.at[at, y + v - 2 * y * v, origin, side]
+        n = 21 + 8 * v + 2 * origin + side
+        return send(block, block, w_s.at[n], w_r.at[n], sib)
 
     def w_begin():
-        g[core, z, x, y] = jnp.zeros((480, LANES), BF16)
-        g[core, z, x, y, 0:240, 0:USED] = wup_in[...].astype(F32).T.astype(BF16)
-        g[core, z, x, y, 240:480, 0:USED] = wdown_in[...]
-        w_y().start()
-
-    def w_here(origin):
-        w_x(origin, x).start()
-        w_core(origin, x, core).start()
-
-    def w_first():
-        w_y().wait_recv()
-
-        @pl.when(z < 3)
-        def _():
-            w_up(1, z).start()
-
-        @pl.when(z > 0)
-        def _():
-            w_down(1, z).start()
-
-        w_here(z)
-
-    def w_step(s):
+        g[core, y, z, x] = jnp.zeros((480, LANES), BF16)
+        g[core, y, z, x, 0:240, 0:USED] = wup_in[...].astype(F32).T.astype(BF16)
+        g[core, y, z, x, 240:480, 0:USED] = wdown_in[...]
+
+    def w_here(v, origin):
+        w_x(v, origin, x).start()
+        w_core(v, origin, x, core).start()
+
+    def w_first(v):
+        if v:
+            w_y().wait_recv()
+        else:
+            w_y().start()
+        pl.when(z < 3)(lambda: w_up(v, 1, z).start())
+        pl.when(z > 0)(lambda: w_down(v, 1, z).start())
+        w_here(v, z)
+
+    def w_step(v, s):
         @pl.when(z >= s)
         def _():
-            w_up(s, z - s).wait_recv()
+            w_up(v, s, z - s).wait_recv()
             if s < 3:
-
-                @pl.when(z < 3)
-                def _():
-                    w_up(s + 1, z - s).start()
-
-            w_here(z - s)
+                pl.when(z < 3)(lambda: w_up(v, s + 1, z - s).start())
+            w_here(v, z - s)
 
         @pl.when(z + s <= 3)
         def _():
-            w_down(s, z + s).wait_recv()
+            w_down(v, s, z + s).wait_recv()
             if s < 3:
-
-                @pl.when(z > 0)
-                def _():
-                    w_down(s + 1, z + s).start()
-
-            w_here(z + s)
-
-    def w_other(s):
+                pl.when(z > 0)(lambda: w_down(v, s + 1, z + s).start())
+            w_here(v, z + s)
+
+    def w_other(v, s):
         def one(origin):
-            w_x(origin, 1 - x).wait_recv()
-            w_core(origin, 1 - x, core).start()
+            w_x(v, origin, 1 - x).wait_recv()
+            w_core(v, origin, 1 - x, core).start()
 
         if s == 0:
             one(z)
@@ -233,23 +224,25 @@
             pl.when(z + s <= 3)(lambda: one(z + s))
 
     def w_end():
-        for origin in range(4):
-            for side in (0, 1):
-                w_core(origin, side, 1 - core).wait_recv()
+        for v in (0, 1):
+            for origin in range(4):
+                for side in (0, 1):
+                    w_core(v, origin, side, 1 - core).wait_recv()
 
     def w_sent():
         w_y().wait_send()
-        for s in (1, 2, 3):
-            pl.when((z >= s - 1) & (z < 3))(lambda: w_up(s, z - s + 1).wait_send())
-            pl.when((z + s - 1 <= 3) & (z > 0))(lambda: w_down(s, z + s - 1).wait_send())
-        for origin in range(4):
-            w_x(origin, x).wait_send()
-            for side in (0, 1):
-                w_core(origin, side, core).wait_send()
+        for v in (0, 1):
+            for s in (1, 2, 3):
+                pl.when((z >= s - 1) & (z < 3))(lambda: w_up(v, s, z - s + 1).wait_send())
+                pl.when((z + s - 1 <= 3) & (z > 0))(lambda: w_down(v, s, z + s - 1).wait_send())
+            for origin in range(4):
+                w_x(v, origin, x).wait_send()
+                for side in (0, 1):
+                    w_core(v, origin, side, core).wait_send()
 
     def assemble():
         def step(i, _):
-            parts = [gw[n % 2, i // 2, i % 2, n // 2] for n in range(4)]
+            parts = [gw[n % 2, n // 2, i // 2, i % 2] for n in range(4)]
             full = nn(jnp.concatenate(parts, axis=1), spread[...]).astype(BF16)
             r = pl.ds(pl.multiple_of(i * 240, 240), 240)
             wup[r, :] = full[0:240]
@@ -260,171 +253,184 @@
 
     order = (3, 0, 2, 1)
 
-    def g_core(origin):
-        return send(
-            g.at[1 - core, origin], rc.at[origin], c_s.at[origin], c_r.at[origin], sib
-        )
-
-    def g_x(origin):
-        return send(
-            g.at[core, origin, 1 - x], rx.at[origin], c_s.at[4 + origin], c_r.at[4 + origin], xpart
-        )
-
-    def g_up(s, to):
-        return send(g.at[core, to, x], rz.at[0, s - 1], c_s.at[7 + s], c_r.at[7 + s], above)
-
-    def g_down(s, to):
-        return send(g.at[core, to, x], rz.at[1, s - 1], c_s.at[10 + s], c_r.at[10 + s], below)
+    def g_core(v, origin):
+        n = 4 * v + origin
+        return send(g.at[1 - core, v, origin], rc.at[v, origin], c_s.at[n], c_r.at[n], sib)
+
+    def g_x(v, origin):
+        n = 8 + 4 * v + origin
+        return send(g.at[core, v, origin, 1 - x], rx.at[v, origin], c_s.at[n], c_r.at[n], xpart)
+
+    def g_up(v, s, to):
+        n = 15 + 3 * v + s
+        return send(g.at[core, v, to, x], rz.at[0, v, s - 1], c_s.at[n], c_r.at[n], above)
+
+    def g_down(v, s, to):
+        n = 21 + 3 * v + s
+        return send(g.at[core, v, to, x], rz.at[1, v, s - 1], c_s.at[n], c_r.at[n], below)
 
     def g_y():
-        return send(g.at[core, z, x, 1 - y], ry, c_s.at[14], c_r.at[14], ypart)
-
-    def add_pair(origin, side, ref):
-        for n in (0, 1):
-            g[core, origin, side, n] = (
-                g[core, origin, side, n].astype(F32) + ref[n].astype(F32)
-            ).astype(BF16)
+        return send(g.at[core, 1 - y, z, x], ry, c_s.at[28], c_r.at[28], ypart)
+
+    def add_block(v, origin, side, ref):
+        g[core, v, origin, side] = (
+            g[core, v, origin, side].astype(F32) + ref[...].astype(F32)
+        ).astype(BF16)
 
     def g_begin():
+        for v in (0, 1):
+            for origin in order:
+                g_core(v, origin).start()
+
+    def g_first(v):
         for origin in order:
-            g_core(origin).start()
-
-    def g_first():
+            g_core(v, origin).wait_recv()
+            add_block(v, origin, 1 - x, rc.at[v, origin, 1 - x])
+            g_x(v, origin).start()
         for origin in order:
-            g_core(origin).wait_recv()
-            add_pair(origin, 1 - x, rc.at[origin, 1 - x])
-            g_x(origin).start()
-        for origin in order:
-            add_pair(origin, x, rc.at[origin, x])
-
-    def g_add_x(origins):
+            add_block(v, origin, x, rc.at[v, origin, x])
+
+    def g_add_x(v, origins):
         for origin in origins:
-            g_x(origin).wait_recv()
-            add_pair(origin, x, rx.at[origin])
-
-    def g_send(s):
-        pl.when(z < s)(lambda: g_up(s, 4 - s + z).start())
-        pl.when(3 - z < s)(lambda: g_down(s, s + z - 4).start())
-
-    def g_recv(s):
+            g_x(v, origin).wait_recv()
+            add_block(v, origin, x, rx.at[v, origin])
+
+    def g_send(v, s):
+        pl.when(z < s)(lambda: g_up(v, s, 4 - s + z).start())
+        pl.when(3 - z < s)(lambda: g_down(v, s, s + z - 4).start())
+
+    def g_recv(v, s):
         @pl.when((z >= 1) & (z <= s))
         def _():
-            g_up(s, 0).wait_recv()
-            add_pair(3 - s + z, x, rz.at[0, s - 1])
+            g_up(v, s, 0).wait_recv()
+            add_block(v, 3 - s + z, x, rz.at[0, v, s - 1])
 
         @pl.when((z <= 2) & (z >= 3 - s))
         def _():
-            g_down(s, 0).wait_recv()
-            add_pair(s + z - 3, x, rz.at[1, s - 1])
+            g_down(v, s, 0).wait_recv()
+            add_block(v, s + z - 3, x, rz.at[1, v, s - 1])
+
+    def g_y_begin(v):
+        pl.when(y != v)(lambda: g_y().start())
 
     def g_last():
         g_y().wait_recv()
-        total = g[core, z, x, y].astype(F32) + ry[...].astype(F32)
+        total = g[core, y, z, x].astype(F32) + ry[...].astype(F32)
         dup[...] = total[0:240].T[0:USED]
         ddown[...] = total[240:480, 0:USED]
-        for n in range(4):
-            g_core(n).wait_send()
-            g_x(n).wait_send()
-        for s in (1, 2, 3):
-            pl.when(z < s)(lambda: g_up(s, 0).wait_send())
-            pl.when(3 - z < s)(lambda: g_down(s, 0).wait_send())
+        for v in (0, 1):
+            for n in range(4):
+                g_core(v, n).wait_send()
+                g_x(v, n).wait_send()
+            for s in (1, 2, 3):
+                pl.when(z < s)(lambda: g_up(v, s, 0).wait_send())
+                pl.when(3 - z < s)(lambda: g_down(v, s, 0).wait_send())
         g_y().wait_send()
 
     spans = ((384, 512), (256, 384), (0, 256))
 
-    def slot_of(n):
-        first, last = spans[n]
-        size = (last - first) // 8
-        return first, size
-
-    def f_part(n, p):
-        first, size = slot_of(n)
-        return pl.ds(pl.multiple_of(first + p * size, 16), size)
-
-    def f_in(n, p):
-        first, size = slot_of(n)
-        return pl.ds(pl.multiple_of(first + p * size, 16), size)
-
-    def f_out_copy(n, p):
+    def f_size(n):
+        return (spans[n][1] - spans[n][0]) // 8
+
+    def f_rows(n, p):
+        return pl.ds(pl.multiple_of(spans[n][0] + p * f_size(n), 16), f_size(n))
+
+    def f_out(n, p, slot):
         return send(
-            wall.at[f_part(n, p)], wsum.at[f_in(n, d)], f_s.at[0, n, p], f_r.at[0, n, d], (p, h)
+            f_send[n].at[p], f_got[n].at[slot], f_s.at[0, n, p], f_r.at[0, n, slot], (p, h)
         )
 
-    def f_in_copy(n, p):
-        return send(
-            wall.at[f_part(n, p)], wsum.at[f_in(n, p)], f_s.at[0, n, p], f_r.at[0, n, p], (p, h)
-        )
-
-    def f_back_copy(n, p, at):
-        return send(
-            wres.at[f_part(n, at)], wres.at[f_part(n, at)], f_s.at[1, n, p], f_r.at[1, n, at], (p, h)
-        )
+    def f_home(n, p, at):
+        rows = wres.at[f_rows(n, at)]
+        return send(rows, rows, f_s.at[1, n, p], f_r.at[1, n, at], (p, h))
 
     def f_begin(n):
-        first, last = spans[n]
-        wall[first:last, :] = acc[first:last, :].astype(BF16)
-        wsum[f_in(n, d), :] = wall[f_part(n, d), :]
+        first, size = spans[n][0], f_size(n)
+        if n == 2:
+            for at in range(3):
+                row = sums[0, at : at + 1, :]
+                top = row.astype(BF16).astype(F32)
+                vecs[2 * at : 2 * at + 1, :] = top
+                vecs[2 * at + 1 : 2 * at + 2, :] = row - top
+            extra = vecs[...].astype(BF16)
+        for p in range(8):
+            f_send[n][p, 0:size, :] = acc[first + p * size : first + (p + 1) * size, :].astype(BF16)
+            if n == 2:
+                f_send[n][p, size : size + 16, :] = extra
+        f_got[n][d] = f_send[n][d]
         for p in peers:
-            f_out_copy(n, p).start()
+            f_out(n, p, d).start()
 
     def f_back(n):
-        first, size = slot_of(n)
+        size = f_size(n)
         for p in peers:
-            f_in_copy(n, p).wait_recv()
-        total = jnp.zeros((size, 512), F32)
-        for p in range(8):
-            total = total + wsum[first + p * size : first + (p + 1) * size, :].astype(F32)
-        wres[f_part(n, d), :] = total.astype(BF16)
+            f_out(n, p, p).wait_recv()
+        total = f_got[n][0].astype(F32)
+        for p in range(1, 8):
+            total = total + f_got[n][p].astype(F32)
+        wres[f_rows(n, d), :] = total[0:size].astype(BF16)
         for p in peers:
-            f_back_copy(n, p, d).start()
+            f_home(n, p, d).start()
+        if n == 2:
+            for at in range(3):
+                row = size + 2 * at
+                sums[0, at : at + 1, :] = total[row : row + 1] + total[row + 1 : row + 2]
+            m_begin(0)
 
     def f_end(n):
         for p in peers:
-            f_back_copy(n, p, p).wait_recv()
+            f_home(n, p, p).wait_recv()
 
     def f_sent(n):
         for p in peers:
-            f_out_copy(n, p).wait_send()
-            f_back_copy(n, p, d).wait_send()
+            f_out(n, p, d).wait_send()
+            f_home(n, p, d).wait_send()
 
     near = (sib, ypart, (d, (h_sib + 2) % 4))
 
     def m_heads(b, n, at):
         return send(sums.at[b], heads_in.at[b, at], m_s.at[b, n], m_r.at[b, at], near[n])
 
-    def m_dp(b, n, at):
-        return send(
-            dp_out.at[b], dp_in.at[b, at], m_s.at[b, 3 + n], m_r.at[b, 4 + at], (peers[n], h)
-        )
+    def m_dp(n, at):
+        return send(dp_out, dp_in.at[at], m_s.at[1, 3 + n], m_r.at[1, 4 + at], (peers[n], h))
 
     def m_begin(b):
         heads_in[b, h] = sums[b]
         for n in range(3):
             m_heads(b, n, h).start()
 
-    def m_middle(b):
+    def m_total(b):
         for n in range(3):
             m_heads(b, n, near[n][1]).wait_recv()
-        total = heads_in[b, 0] + heads_in[b, 1] + heads_in[b, 2] + heads_in[b, 3]
-        if b == 0:
-            row = lax.broadcasted_iota(jnp.int32, total.shape, 0)
-            total = jnp.where(row == 2, sums[b], total)
-        dp_out[b] = total
-        dp_in[b, d] = total
+        return heads_in[b, 0] + heads_in[b, 1] + heads_in[b, 2] + heads_in[b, 3]
+
+    def m_middle():
+        dp_out[...] = m_total(1)
+        dp_in[d] = dp_out[...]
         for n in range(7):
-            m_dp(b, n, d).start()
-
-    def m_end(b):
+            m_dp(n, d).start()
+
+    def m_end():
         for n in range(7):
-            m_dp(b, n, peers[n]).wait_recv()
-        total = dp_in[b, 0]
+            m_dp(n, peers[n]).wait_recv()
+        total = dp_in[0]
         for p in range(1, 8):
-            total = total + dp_in[b, p]
-        small[8 * b : 8 * b + 8, :] = total
+            total = total + dp_in[p]
+        small[8:16, :] = total
         for n in range(3):
-            m_heads(b, n, h).wait_send()
+            m_heads(1, n, h).wait_send()
         for n in range(7):
-            m_dp(b, n, d).wait_send()
+            m_dp(n, d).wait_send()
+
+    def m_last():
+        total = m_total(0)
+        small[0:8, :] = total
+        small[0:1, 0:width] = (
+            total[0:1, 0:width] - attn_bias[...] * total[1:2, 0:width]
+        ) / attn_gain[...]
+        small[2:3, :] = sums[0, 2:3, :]
+        for n in range(3):
+            m_heads(0, n, h).wait_send()
 
     def rows_of(k):
         return slice(k * BLOCK, (k + 1) * BLOCK)
@@ -438,21 +444,35 @@
         pl.semaphore_signal(barrier, inc=1, device_id=other, device_id_type=MESH)
 
     def first_norm(k):
-        xhat, _ = norm(tok[rows_of(k), :].astype(F32))
+        tok_in(k).wait()
+        x_ = result[:, rows_of(k)].astype(F32).T
+        tok[rows_of(k), :] = x_.astype(BF16)
+        xhat, _ = norm(x_)
         n1[k, h, :, 0:width] = (xhat * attn_gain[...] + attn_bias[...]).astype(BF16)
         n1[k, h, :, width:512] = jnp.zeros((BLOCK, 512 - width), BF16)
 
+    def tok_in(k):
+        cols = pl.ds(k * BLOCK, BLOCK)
+        return pltpu.make_async_copy(tok_hbm.at[:, cols], result.at[:, cols], in_s.at[k])
+
+    grad_in = pltpu.make_async_copy(grad_hbm, grad_t, in_s.at[groups])
+    for k in range(groups):
+        tok_in(k).start()
+    grad_in.start()
     first_norm(0)
     pl.semaphore_wait(barrier, len(greeted))
     gather_start(0, n1, 0)
     if inner:
         w_begin()
+        w_first(0)
     for k in range(1, groups):
         first_norm(k)
         gather_start(0, n1, k)
 
     wq[0:width, :] = nn(wqkv[...], perm[...]).astype(BF16)
     wq[width:512, :] = jnp.zeros((512 - width, 3 * LANES), BF16)
+    wqt[:, 0:width] = dims(perm[...], wqkv[...], 0, 1).astype(BF16)
+    wqt[:, width:512] = jnp.zeros((3 * LANES, 512 - width), BF16)
     qkv_b[...] = dims(qkv_bias[...], perm[...].astype(F32), 1, 0, lax.Precision.HIGHEST)
     wo[:, width:512] = jnp.zeros((LANES, 512 - width), BF16)
     wo[:, 0:width] = jnp.concatenate(
@@ -551,7 +571,6 @@
                 inv = jnp.where(head_lanes(BLOCK, j), one, inv)
                 s = later
             ctx[k, r, :] = out
-            ctxb[k, r, :] = out.astype(BF16)
             invl[k, r, :] = inv
             p_out(k, i).start()
             return 0
@@ -561,11 +580,23 @@
     def out_part(k):
         def part(i):
             r = pl.ds(pl.multiple_of(i * BLOCK, BLOCK), BLOCK)
-            return nn(ctxb[k, r, :], wo[...])
+            return nn(ctx[k, r, :].astype(BF16), wo[...])
 
         return part
 
+    if inner:
+        first, step, other = (
+            (lambda *a, f=f: partial(f, *a)) for f in (w_first, w_step, w_other)
+        )
+        w_plan = (
+            {1: [first(1), step(0, 2)], 3: [step(1, 1), step(0, 3)]},
+            {0: [step(1, 2), other(0, 0), other(0, 1), other(1, 0)],
+             2: [step(1, 3), other(0, 2), other(1, 1)]},
+            {0: [other(0, 3), other(1, 2)], 2: [other(1, 3)]},
+        )
     gather_forward(0, n1, 0)
+    if inner:
+        w_step(0, 1)
     for k in range(groups):
         gather_finish(0, n1, k)
         project(k)
@@ -575,14 +606,8 @@
         if k + 1 < groups:
             hooks[3] = [partial(gather_forward, 0, n1, k + 1)]
         if inner:
-            if k == 0:
-                hooks[0] = [w_first]
-                hooks[3] += [partial(w_step, 1), partial(w_other, 0)]
-            if k == 1:
-                hooks[2] = [partial(w_step, 2), partial(w_other, 1)]
-            if k == 2:
-                hooks[0] = [partial(w_step, 3), partial(w_other, 2)]
-                hooks[3] = [partial(w_other, 3)]
+            for at, todo in w_plan[k].items():
+                hooks.setdefault(at, []).extend(todo)
         attend(k, hooks)
         sum_start(0, k, out_part(k))
     sum_forward(0, groups - 1)
@@ -596,6 +621,8 @@
     if inner:
         w_sent()
 
+    grad_in.wait()
+
     def weight_of(k):
         ends = ends_of(k)
         row = lax.broadcasted_iota(jnp.int32, (BLOCK, 1), 0) + h * BLOCK
@@ -610,6 +637,7 @@
         mid[r, :] = middle
         xhat, _ = norm(middle)
         n2[r, 0:width] = (xhat * ffn_gain[...] + ffn_bias[...]).astype(BF16)
+        grad[r, :] = grad_t[:, r].astype(F32).T.astype(BF16)
         d_ffn = (grad[r, :].astype(F32) * weight_of(k)).astype(BF16)
         df[r, 0:width] = d_ffn
         add_sum(15, jnp.sum(d_ffn.astype(F32), axis=0, keepdims=True))
@@ -647,8 +675,8 @@
                     for n in range(4):
                         new = wide[side * 240 : side * 240 + 240, n * LANES : (n + 1) * LANES]
                         if first > 0:
-                            new = new + gg[n % 2, t, side, n // 2, fr, :].astype(F32)
-                        gg[n % 2, t, side, n // 2, fr, :] = new.astype(BF16)
+                            new = new + gg[n % 2, n // 2, t, side, fr, :].astype(F32)
+                        gg[n % 2, n // 2, t, side, fr, :] = new.astype(BF16)
             return 0
 
         lax.fori_loop(0, 4, step, 0)
@@ -656,14 +684,14 @@
     def ffn_post(k):
         r = rows_of(k)
         middle = mid[r, :]
-        result[r, :] = (middle + facc[r, 0:width] + down_bias[...]).astype(BF16)
+        result[:, r] = (middle + facc[r, 0:width] + down_bias[...]).T.astype(BF16)
         g_ = dn2[r, 0:width]
         xhat, rstd = norm(middle)
         add_sum(13, jnp.sum(g_ * xhat, axis=0, keepdims=True))
         add_sum(14, jnp.sum(g_, axis=0, keepdims=True))
         d_result = grad[r, :].astype(F32) * weight_of(k)
         d_middle = d_result + norm_back(g_, ffn_gain[...], xhat, rstd)
-        dtok[r, :] = d_middle
+        mid[r, :] = d_middle
         low = d_middle.astype(BF16)
         da[k, h, :, 0:width] = low
         add_sum(12, jnp.sum(low.astype(F32), axis=0, keepdims=True))
@@ -693,7 +721,7 @@
             do_s[r, :] = g_
             dot_t[:, r] = g_.astype(F32).T
             q_t[:, r] = q_s[k, r, :].astype(F32).T
-            acc[3 * LANES : 4 * LANES, :] += tn(ctxb[k, r, :], da[k, i])
+            acc[3 * LANES : 4 * LANES, :] += tn(ctx[k, r, :].astype(BF16), da[k, i])
             return 0
 
         lax.fori_loop(0, steps, step, 0)
@@ -728,7 +756,8 @@
                 out = jnp.where(head_lanes(BLOCK, j), nn(ds, keys), out)
                 hs = slice(j * HD, (j + 1) * HD)
                 dk_t[hs, :] += nn(q_t[hs, r].astype(BF16), ds)
-                dv_t[hs, :] += nn(dot_t[hs, r].astype(BF16), e)
+                if k < groups - 1:
+                    dv_t[hs, :] += nn(dot_t[hs, r].astype(BF16), e)
                 dp = later
             dq[r, :] = out
 
@@ -748,13 +777,45 @@
             a = a * c - partner(a) * s
             b = dk_t[:, r].T * (1.0 / LOG2E)
             b = b * c - partner(b) * s
-            g_ = jnp.concatenate([a, b, dv_t[:, r].T], axis=1).astype(BF16)
-            dqkv[r, :] = g_
+            if k < groups - 1:
+                g_ = jnp.concatenate([a, b, dv_t[:, r].T], axis=1).astype(BF16)
+            else:
+                g_ = jnp.concatenate([a, b], axis=1).astype(BF16)
+            cols = g_.shape[1]
+            dqkv[r, 0:cols] = g_
             add_sum(2, jnp.sum(g_.astype(F32), axis=0, keepdims=True))
-            acc[0 : 3 * LANES, :] += tn(g_, n1[k, i])
+            acc[0:cols, :] += tn(g_, n1[k, i])
             return 0
 
         lax.fori_loop(0, steps, step, 0)
+
+    def back_values(k):
+        def step(i, _):
+            n = k * steps + i
+            slot = n % 2
+            p_in(n).wait()
+            r = pl.ds(pl.multiple_of(i * BLOCK, BLOCK), BLOCK)
+            for j in range(HEADS):
+                hs = slice(j * HD, (j + 1) * HD)
+                dv_t[hs, :] += nn(dot_t[hs, r].astype(BF16), pslot[slot, j])
+            p_in(k * steps + (i + 2) % steps).start()
+            return 0
+
+        lax.fori_loop(0, steps, step, 0)
+
+        def post(i, _):
+            r = pl.ds(pl.multiple_of(i * BLOCK, BLOCK), BLOCK)
+            g_ = dv_t[:, r].T.astype(BF16)
+            dqkv[r, 2 * LANES : 3 * LANES] = g_
+            sums[0, 2:3, 2 * LANES : 3 * LANES] += jnp.sum(g_.astype(F32), axis=0, keepdims=True)
+            acc[2 * LANES : 3 * LANES, :] += tn(g_, n1[k, i])
+            return 0
+
+        lax.fori_loop(0, steps, post, 0)
+
+    def norm_sums():
+        add_sum(0, jnp.sum(acc[0 : 3 * LANES, :] * wqt[...].astype(F32), axis=0, keepdims=True))
+        add_sum(1, dims(sums[0, 2:3, 0 : 3 * LANES], wqt[...].astype(F32), 1, 0, lax.Precision.HIGHEST))
 
     def tokens_part(i):
         r = pl.ds(pl.multiple_of(i * BLOCK, BLOCK), BLOCK)
@@ -764,53 +825,63 @@
         r = rows_of(k)
         g_ = sum_finish(1, k)[:, 0:width]
         xhat, rstd = norm(tok[r, :].astype(F32))
-        add_sum(0, jnp.sum(g_ * xhat, axis=0, keepdims=True))
-        add_sum(1, jnp.sum(g_, axis=0, keepdims=True))
-        dtok[r, :] += norm_back(g_, attn_gain[...], xhat, rstd)
-
-    for k in range(groups - 1):
-        gather_forward(1, da, k)
+        dtok_out[:, r] = (mid[r, :] + norm_back(g_, attn_gain[...], xhat, rstd)).T
+
+    if inner:
+        wait_x, go, take, first = (
+            (lambda *a, f=f: partial(f, *a)) for f in (g_add_x, g_send, g_recv, g_first)
+        )
+        a, b = order[:2], order[2:]
+        g_plan = (
+            {0: [first(0)], 1: [first(1), m_middle], 3: [wait_x(0, a), go(0, 1)]},
+            {0: [wait_x(0, b), take(0, 1), go(0, 2), m_end],
+             2: [wait_x(1, a), go(1, 1), take(0, 2), go(0, 3)]},
+            {0: [take(0, 3), partial(g_y_begin, 0), wait_x(1, b), take(1, 1), go(1, 2)],
+             2: [take(1, 2), go(1, 3), partial(f_back, 0)],
+             3: [partial(f_back, 1)]},
+        )
+    gather_forward(1, da, 0)
     for k in range(groups):
         gather_finish(1, da, k)
         back_prep(k)
         if k > 0:
             sum_forward(1, k - 1)
+        if k == groups - 1:
+            if inner:
+                f_begin(0)
+            back_values(k)
+            if inner:
+                f_begin(1)
         hooks = {}
         if k == 0:
-            hooks[1] = [partial(gather_forward, 1, da, groups - 1)]
+            hooks[1] = [partial(gather_forward, 1, da, 1)]
+            hooks[3] = [partial(gather_forward, 1, da, 2)]
         if inner:
-            if k == 0:
-                hooks[0] = [g_first, partial(m_middle, 1)]
-            if k == 1:
-                hooks[0] = [partial(g_add_x, order[:2]), partial(g_send, 1), partial(m_end, 1)]
-                hooks[3] = [partial(g_add_x, order[2:]), partial(g_recv, 1), partial(g_send, 2)]
-            if k == 2:
-                hooks[0] = [partial(f_begin, 0)]
-                hooks[1] = [partial(g_recv, 2), partial(g_send, 3)]
-                hooks[2] = [partial(f_back, 0)]
-                hooks[3] = [partial(g_recv, 3), g_y().start]
+            for at, todo in g_plan[k].items():
+                hooks.setdefault(at, []).extend(todo)
         back(k, hooks)
         back_post(k)
+        if k == groups - 1:
+            norm_sums()
         if inner and k == groups - 1:
-            f_begin(1)
             f_begin(2)
         sum_start(1, k, tokens_part)
     for k in range(groups - 1):
         last_norm(k)
+    if inner:
+        g_recv(1, 3)
+        g_y_begin(1)
     sum_forward(1, groups - 1)
     if inner:
-        f_back(1)
         f_back(2)
     last_norm(groups - 1)
     if inner:
-        m_begin(0)
         g_last()
-        m_middle(0)
         for n in range(3):
             f_end(n)
         dwqkv[...] = dims(wres[0 : 3 * LANES, :], perm[...], 0, 1)[0:width]
         dwout[...] = wres[3 * LANES : 4 * LANES, :].astype(F32)[0:USED, 0:width]
-        m_end(0)
+        m_last()
         for n in range(3):
             f_sent(n)
     else:
@@ -864,7 +935,7 @@
     shape = jax.ShapeDtypeStruct
     row = lambda v: v.reshape(1, -1)
     v, dma = pltpu.VMEM, pltpu.SemaphoreType.DMA
-    chunks = (2, 4, 2, 2, 480, LANES)
+    chunks = (2, 2, 4, 2, 480, LANES)
     if inner:
         first = (
             shape((width, 3 * USED), F32),
@@ -874,20 +945,21 @@
         )
         remote = [
             v(chunks, BF16),
-            v((4, 2, 2, 480, LANES), BF16),
-            v((4, 2, 480, LANES), BF16),
-            v((2, 3, 2, 480, LANES), BF16),
+            v((2, 4, 2, 480, LANES), BF16),
+            v((2, 4, 480, LANES), BF16),
+            v((2, 2, 3, 480, LANES), BF16),
             v((480, LANES), BF16),
+            [v((8, n, 512), BF16) for n in (16, 16, 48)],
+            [v((8, n, 512), BF16) for n in (16, 16, 48)],
             v((4 * LANES, 512), BF16),
-            v((4 * LANES, 512), BF16),
-            v((4 * LANES, 512), BF16),
+            v((16, 512), F32),
             v((2, 4, 8, 512), F32),
-            v((2, 8, 512), F32),
-            v((2, 8, 8, 512), F32),
-            dma((19,)),
-            dma((19,)),
-            dma((15,)),
-            dma((15,)),
+            v((8, 512), F32),
+            v((8, 8, 512), F32),
+            dma((37,)),
+            dma((37,)),
+            dma((29,)),
+            dma((29,)),
             dma((2, 3, 8)),
             dma((2, 3, 8)),
             dma((2, 10)),
@@ -899,24 +971,28 @@
     return pl.pallas_call(
         partial(body, inner),
         out_shape=(
-            shape((own, width), BF16),
-            shape((own, width), F32),
+            shape((width, own), BF16),
+            shape((width, own), F32),
             first,
             shape((16, 512), F32),
             shape((groups, 4, HEADS, BLOCK, group_rows), BF16),
         ),
-        in_specs=[vm] * 4 + [[vm] * len(w_in)] + [vm] * 12 + [sm] * 3,
+        in_specs=[anywhere] * 2 + [vm] * 2 + [[vm] * len(w_in)] + [vm] * 12 + [sm] * 3,
         out_specs=(vm, vm, (vm,) * len(first), vm, anywhere),
         scratch_shapes=[
+            v((width, own), BF16),
+            v((own, width), BF16),
+            v((own, width), BF16),
+            dma((groups + 1,)),
             v((groups, 4, BLOCK, 512), BF16),
             v((512, 3 * LANES), BF16),
+            v((3 * LANES, 512), BF16),
             v((LANES, 512), BF16),
             v((1, 3 * LANES), F32),
             v((groups, group_rows, LANES), BF16),
             v((groups, group_rows, LANES), BF16),
             v((groups, group_rows, LANES), BF16),
             v((groups, group_rows, LANES), F32),
-            v((groups, group_rows, LANES), BF16),
             v((groups, group_rows, LANES), F32),
             v((2, HEADS, BLOCK, group_rows), BF16),
             v((groups, 2, BLOCK, 512), BF16),
@@ -955,7 +1031,7 @@
         ),
         name="layer",
     )(
-        tokens, grad, wqkv, wout, w_in, row(attn_gain), row(attn_bias), row(qkv_bias),
+        tokens.T, grad.T, wqkv, wout, w_in, row(attn_gain), row(attn_bias), row(qkv_bias),
         row(out_bias), row(ffn_gain), row(ffn_bias), up_bias.reshape(4, 480), row(down_bias),
         jnp.asarray(permutation(), BF16), jnp.asarray(spreading(), BF16), jnp.asarray(c),
         jnp.asarray(s), lengths, ids, cw,
@@ -978,7 +1054,7 @@
         part = lax.all_gather(part, "heads", axis=0)
         part = jnp.pad(part, ((0, 0),) * 3 + ((0, LANES - USED),))
         part = part.reshape(2, 2, 2, 4, 2, 240, LANES)
-        w_in = [part.transpose(1, 3, 4, 0, 2, 5, 6).reshape(2, 4, 2, 2, 480, LANES)]
+        w_in = [part.transpose(1, 0, 3, 4, 2, 5, 6).reshape(2, 2, 4, 2, 480, LANES)]
     result, dtok, first, small, _ = layer(
         inner, tokens, qkv_weight, out_weight, w_in, attn_norm_gain, attn_norm_bias,
         qkv_bias, out_bias, ffn_norm_gain, ffn_norm_bias, up_bias, down_bias, lengths,
@@ -990,7 +1066,9 @@
         acc, grads = first
         acc, own_sums = lax.psum((acc, small[2]), "dp")
         small = lax.psum(small, ("dp", "heads")).at[2].set(own_sums)
-        grads = grads.reshape(2, 4, 2, 2, 2, 240, LANES).transpose(3, 0, 4, 1, 2, 5, 6)
+        gain_sum = (small[0, :width] - attn_norm_bias * small[1, :width]) / attn_norm_gain
+        small = small.at[0, :width].set(gain_sum)
+        grads = grads.reshape(2, 2, 4, 2, 2, 240, LANES).transpose(1, 0, 4, 2, 3, 5, 6)
         grads = grads.reshape(4, 2, ff, LANES)[..., :USED]
         grads = lax.psum_scatter(grads, "heads", scatter_dimension=0).astype(F32)
         grads = lax.psum_scatter(grads, "dp", scatter_dimension=1, tiled=True)
@@ -1001,7 +1079,7 @@
     dqkvb = small[2, : 3 * LANES].reshape(3, LANES)[:, :USED].reshape(3, HEADS, HD)
     dqkvb = dqkvb.transpose(1, 0, 2).reshape(-1)
     return (
-        result, dtok, small[0, :width], small[1, :width], dwqkv, dqkvb, dwout,
+        result.T, dtok.T, small[0, :width], small[1, :width], dwqkv, dqkvb, dwout,
         small[12, :width], small[13, :width], small[14, :width], dup,
         small[8:12, :480].reshape(ff), ddown, small[15, :width],
     )

time: 187 us -> 176 us (0.941)
  Pallas kernels: 168 us -> 161 us
  local copies, waits for them, and re-layouts: 17.3 us -> 13.6 us
    pallas_call x1, Pallas kernels: 168 us -> 161 us  [layer(): pl.pallas_call(partial(body, inner), out_shape=(shape((width, own), BF16)...]
    unnamed x20 -> x16, local copies, waits for them, and re-layouts: 10.3 us -> 6.5 us
where the time goes in v3:
time: 176 us
  Pallas kernels  161 us (91%)
  local copies, waits for them, and re-layouts  13.6 us (8%)
    pallas_call x1, Pallas kernels, layer(): pl.pallas_call(partial(body, inner), out_shape=(shape((width, own), BF16)...  161 us
    unnamed x16, local copies, waits for them, and re-layouts  6.5 us

profile of v3, /device:TPU:0, one launch (start us, length us, event | category | flops | bytes accessed | tf_op | source)
XLA Modules:
  0.0 175.7 jit_solution(1656429506271354357)
XLA Ops:
  0.6 1.2 reshape.63.qkv_bias
  1.9 1.4 reshape.67.up_bias
  3.3 161.5 %layer.1 = (bf16[480,768]{1,0:T(8,128)(2,1)}, f32[480,768]{1,0:T(8,128)}, f32[480,360]{1,0:T(8,128)}, f32[120,480]{1,0:T(8,128)}, f32[120,240]{1,0:T(8,128)}, /*...) custom-call(bf16[480,768]{1,0:T(8,128)(2,1)} %bitcast.20, bf16[480,768]{1,0:T(8,128)(2,1)} %bitcast.21, ...), custom_call_target="tpu_custom_call" | custom-call | tf_op jit(solution)/shard_map/layer/pallas_call | solution.py:971
  164.8 0.0 copy-start
  164.8 0.8 slice_reduce_fusion
  165.6 0.7 slice.34
  166.3 1.5 fusion
  167.8 0.7 reshape.71
  168.5 0.1 reshape.69
  168.6 0.7 reshape.70
  169.2 2.0 %copy.42 = bf16[768,480]{0,1:T(8,128)(2,1)} copy(bf16[768,480]{0,1:T(8,128)(2,1)} %bitcast.22) | data formatting | bytes 1474560
  171.3 0.0 copy-done
  171.3 0.0 copy-start.1
  171.3 0.0 copy-start.2
  171.3 1.1 copy.43
  172.4 0.5 copy-done.1
  172.9 0.0 copy-start.4
  172.9 0.0 copy-start.3
  172.9 0.9 copy.44
  173.7 0.0 copy-done.2
  173.7 0.7 copy.45
  174.4 0.0 copy-done.4
  174.4 0.6 copy.46
  175.1 0.0 copy-done.3
  175.1 0.6 copy.47
  (1 shorter events, 0.0 us)
Async XLA Ops:
  164.8 6.5 %copy-start = (f32[480,768]{1,0:T(8,128)S(1)}, f32[480,768]{1,0:T(8,128)}, u32[]{:S(2)}) copy-start(f32[480,768]{1,0:T(8,128)} %get-tuple-element.22) | copy-start | bytes 4423684
  171.3 1.6 copy-start.1
  171.3 2.5 %copy-start.2 = (f32[120,480]{1,0:T(8,128)S(1)}, f32[120,480]{1,0:T(8,128)}, u32[]{:S(2)}) copy-start(f32[120,480]{1,0:T(8,128)} %get-tuple-element.54) | copy-start | bytes 691204
  172.9 1.6 copy-start.4
  172.9 2.2 %copy-start.3 = (f32[240,120]{1,0:T(8,128)S(1)}, f32[240,120]{1,0:T(8,128)}, u32[]{:S(2)}) copy-start(f32[240,120]{1,0:T(8,128)} %get-tuple-element.60) | copy-start | bytes 345604

commit v4 on v3

--- a/solution.py
+++ b/solution.py
@@ -833,11 +833,13 @@
         )
         a, b = order[:2], order[2:]
         g_plan = (
-            {0: [first(0)], 1: [first(1), m_middle], 3: [wait_x(0, a), go(0, 1)]},
-            {0: [wait_x(0, b), take(0, 1), go(0, 2), m_end],
-             2: [wait_x(1, a), go(1, 1), take(0, 2), go(0, 3)]},
-            {0: [take(0, 3), partial(g_y_begin, 0), wait_x(1, b), take(1, 1), go(1, 2)],
-             2: [take(1, 2), go(1, 3), partial(f_back, 0)],
+            {0: [first(0)], 1: [first(1)], 3: [wait_x(0, a), go(0, 1)]},
+            {0: [wait_x(0, b), take(0, 1), go(0, 2), m_middle],
+             1: [wait_x(1, a), go(1, 1)],
+             2: [take(0, 2), go(0, 3)],
+             3: [wait_x(1, b), take(1, 1), go(1, 2)]},
+            {0: [take(0, 3), partial(g_y_begin, 0), take(1, 2), go(1, 3)],
+             2: [take(1, 3), partial(g_y_begin, 1), partial(f_back, 0), m_end],
              3: [partial(f_back, 1)]},
         )
     gather_forward(1, da, 0)
@@ -868,9 +870,6 @@
         sum_start(1, k, tokens_part)
     for k in range(groups - 1):
         last_norm(k)
-    if inner:
-        g_recv(1, 3)
-        g_y_begin(1)
     sum_forward(1, groups - 1)
     if inner:
         f_back(2)

time: 176 us -> 166 us (0.943)
  Pallas kernels: 161 us -> 151 us
    pallas_call x1, Pallas kernels: 161 us -> 151 us  [layer(): pl.pallas_call(partial(body, inner), out_shape=(shape((width, own), BF16)...]
where the time goes in v4:
time: 166 us
  Pallas kernels  151 us (91%)
  local copies, waits for them, and re-layouts  13.6 us (8%)
    pallas_call x1, Pallas kernels, layer(): pl.pallas_call(partial(body, inner), out_shape=(shape((width, own), BF16)...  151 us
    unnamed x16, local copies, waits for them, and re-layouts  6.5 us

profile of v4, /device:TPU:0, one launch (start us, length us, event | category | flops | bytes accessed | tf_op | source)
XLA Modules:
  0.0 165.7 jit_solution(10206433683558759214)
XLA Ops:
  0.6 1.2 reshape.63.qkv_bias
  1.9 1.4 reshape.67.up_bias
  3.3 151.4 %layer.1 = (bf16[480,768]{1,0:T(8,128)(2,1)}, f32[480,768]{1,0:T(8,128)}, f32[480,360]{1,0:T(8,128)}, f32[120,480]{1,0:T(8,128)}, f32[120,240]{1,0:T(8,128)}, /*...) custom-call(bf16[480,768]{1,0:T(8,128)(2,1)} %bitcast.20, bf16[480,768]{1,0:T(8,128)(2,1)} %bitcast.21, ...), custom_call_target="tpu_custom_call" | custom-call | tf_op jit(solution)/shard_map/layer/pallas_call | solution.py:970
  154.7 0.0 copy-start
  154.7 0.8 slice_reduce_fusion
  155.6 0.7 slice.34
  156.3 1.5 fusion
  157.7 0.7 reshape.71
  158.4 0.1 reshape.69
  158.5 0.7 reshape.70
  159.2 2.0 %copy.42 = bf16[768,480]{0,1:T(8,128)(2,1)} copy(bf16[768,480]{0,1:T(8,128)(2,1)} %bitcast.22) | data formatting | bytes 1474560
  161.2 0.0 copy-done
  161.2 0.0 copy-start.1
  161.2 0.0 copy-start.2
  161.2 1.1 copy.43
  162.3 0.5 copy-done.1
  162.8 0.0 copy-start.4
  162.8 0.0 copy-start.3
  162.8 0.9 copy.44
  163.7 0.0 copy-done.2
  163.7 0.7 copy.45
  164.4 0.0 copy-done.4
  164.4 0.6 copy.46
  165.0 0.0 copy-done.3
  165.0 0.6 copy.47
  (1 shorter events, 0.0 us)
Async XLA Ops:
  154.7 6.5 %copy-start = (f32[480,768]{1,0:T(8,128)S(1)}, f32[480,768]{1,0:T(8,128)}, u32[]{:S(2)}) copy-start(f32[480,768]{1,0:T(8,128)} %get-tuple-element.22) | copy-start | bytes 4423684
  161.2 1.6 copy-start.1
  161.2 2.5 %copy-start.2 = (f32[120,480]{1,0:T(8,128)S(1)}, f32[120,480]{1,0:T(8,128)}, u32[]{:S(2)}) copy-start(f32[120,480]{1,0:T(8,128)} %get-tuple-element.54) | copy-start | bytes 691204
  162.8 1.6 copy-start.4
  162.8 2.2 %copy-start.3 = (f32[240,120]{1,0:T(8,128)S(1)}, f32[240,120]{1,0:T(8,128)}, u32[]{:S(2)}) copy-start(f32[240,120]{1,0:T(8,128)} %get-tuple-element.60) | copy-start | bytes 345604

commit v5 on v4

--- a/solution.py
+++ b/solution.py
@@ -71,8 +71,8 @@
 
 
 def body(
-    inner, tok_hbm, grad_hbm, wqkv, wout, w_in, attn_gain, attn_bias, qkv_bias, out_bias, ffn_gain,
-    ffn_bias, up_bias, down_bias, perm, spread, cos, sin, lengths, ids, cw,
+    inner, tok_hbm, grad_hbm, wqkv, wout, w_in, attn_gain, attn_bias, out_bias, ffn_gain,
+    ffn_bias, wide_bias, down_bias, perm, spread, cos, sin, lengths, ids, cw,
     result, dtok_out, d_first, small, phbm,
     grad_t, tok, grad, in_s,
     n1, wq, wqt, wo, qkv_b, q_s, k_s, v_s, ctx, invl, pslot,
@@ -428,7 +428,9 @@
         small[0:1, 0:width] = (
             total[0:1, 0:width] - attn_bias[...] * total[1:2, 0:width]
         ) / attn_gain[...]
-        small[2:3, :] = sums[0, 2:3, :]
+        small[2:3, 0 : 3 * USED] = dims(
+            sums[0, 2:3, 0 : 3 * LANES], perm[...].astype(F32), 1, 1, lax.Precision.HIGHEST
+        )
         for n in range(3):
             m_heads(0, n, h).wait_send()
 
@@ -473,7 +475,9 @@
     wq[width:512, :] = jnp.zeros((512 - width, 3 * LANES), BF16)
     wqt[:, 0:width] = dims(perm[...], wqkv[...], 0, 1).astype(BF16)
     wqt[:, width:512] = jnp.zeros((3 * LANES, 512 - width), BF16)
-    qkv_b[...] = dims(qkv_bias[...], perm[...].astype(F32), 1, 0, lax.Precision.HIGHEST)
+    qkv_b[...] = dims(
+        wide_bias[4:5, 0 : 3 * USED], perm[...].astype(F32), 1, 0, lax.Precision.HIGHEST
+    )
     wo[:, width:512] = jnp.zeros((LANES, 512 - width), BF16)
     wo[:, 0:width] = jnp.concatenate(
         [wout[...].astype(F32), jnp.zeros((LANES - USED, width), F32)], axis=0
@@ -650,7 +654,7 @@
         def step(t, _):
             f = pl.ds(pl.multiple_of(t * 480, 480), 480)
             wu, wd = wup[f, :], wdown[f, :]
-            u = nt(n2[r, :], wu) + up_bias[pl.ds(t, 1), :]
+            u = nt(n2[r, :], wu) + wide_bias[pl.ds(t, 1), :]
             phi = 0.5 + 0.5 * lax.erf(u * (0.5**0.5))
             hid = (u * phi).astype(BF16)
             slope = phi + u * (jnp.exp(u * u * -0.5) * 0.3989422804014327)
@@ -933,6 +937,7 @@
     anywhere = pl.BlockSpec(memory_space=pl.ANY)
     shape = jax.ShapeDtypeStruct
     row = lambda v: v.reshape(1, -1)
+    wide_bias = jnp.concatenate([up_bias, jnp.pad(qkv_bias, (0, 480 - 3 * USED))]).reshape(5, 480)
     v, dma = pltpu.VMEM, pltpu.SemaphoreType.DMA
     chunks = (2, 2, 4, 2, 480, LANES)
     if inner:
@@ -976,7 +981,7 @@
             shape((16, 512), F32),
             shape((groups, 4, HEADS, BLOCK, group_rows), BF16),
         ),
-        in_specs=[anywhere] * 2 + [vm] * 2 + [[vm] * len(w_in)] + [vm] * 12 + [sm] * 3,
+        in_specs=[anywhere] * 2 + [vm] * 2 + [[vm] * len(w_in)] + [vm] * 11 + [sm] * 3,
         out_specs=(vm, vm, (vm,) * len(first), vm, anywhere),
         scratch_shapes=[
             v((width, own), BF16),
@@ -1030,8 +1035,8 @@
         ),
         name="layer",
     )(
-        tokens.T, grad.T, wqkv, wout, w_in, row(attn_gain), row(attn_bias), row(qkv_bias),
-        row(out_bias), row(ffn_gain), row(ffn_bias), up_bias.reshape(4, 480), row(down_bias),
+        tokens.T, grad.T, wqkv, wout, w_in, row(attn_gain), row(attn_bias), row(out_bias),
+        row(ffn_gain), row(ffn_bias), wide_bias, row(down_bias),
         jnp.asarray(permutation(), BF16), jnp.asarray(spreading(), BF16), jnp.asarray(c),
         jnp.asarray(s), lengths, ids, cw,
     )
@@ -1075,8 +1080,11 @@
         dwqkv = acc[: 3 * LANES, :width].reshape(3, LANES, width)[:, :USED]
         dwqkv = dwqkv.reshape(3, HEADS, HD, width).transpose(3, 1, 0, 2).reshape(width, 3 * USED)
         dwout = acc[3 * LANES : 3 * LANES + USED, :width]
-    dqkvb = small[2, : 3 * LANES].reshape(3, LANES)[:, :USED].reshape(3, HEADS, HD)
-    dqkvb = dqkvb.transpose(1, 0, 2).reshape(-1)
+    if inner:
+        dqkvb = small[2, : 3 * USED]
+    else:
+        dqkvb = small[2, : 3 * LANES].reshape(3, LANES)[:, :USED].reshape(3, HEADS, HD)
+        dqkvb = dqkvb.transpose(1, 0, 2).reshape(-1)
     return (
         result.T, dtok.T, small[0, :width], small[1, :width], dwqkv, dqkvb, dwout,
         small[12, :width], small[13, :width], small[14, :width], dup,

time: 166 us -> 166 us (level)
  local copies, waits for them, and re-layouts: 13.6 us -> 11.8 us
    reshape x4 -> x1, local copies, waits for them, and re-layouts: 3.37 us -> 0.68 us  [layer(): jnp.concatenate([up_bias, jnp.pad(qkv_bias, (0, 480 - 3 * USED))])]
where the time goes in v5:
time: 166 us; the launch traced here: 165 us
  Pallas kernels  152 us (92%)
  local copies, waits for them, and re-layouts  11.8 us (7%)
    pallas_call x1, Pallas kernels, layer(): pl.pallas_call(partial(body, inner), out_shape=(shape((width, own), BF16)...  152 us
    unnamed x16, local copies, waits for them, and re-layouts  6.81 us

profile of v5, /device:TPU:0, one launch (start us, length us, event | category | flops | bytes accessed | tf_op | source)
XLA Modules:
  0.0 165.3 jit_solution(15906186803776880599)
XLA Ops:
  0.6 0.7 select_maximum_fusion
  1.4 0.7 reshape.57.wide_bias
  2.0 152.1 %layer.1 = (bf16[480,768]{1,0:T(8,128)(2,1)}, f32[480,768]{1,0:T(8,128)}, f32[480,360]{1,0:T(8,128)}, f32[120,480]{1,0:T(8,128)}, f32[120,240]{1,0:T(8,128)}, /*...) custom-call(bf16[480,768]{1,0:T(8,128)(2,1)} %bitcast.17, bf16[480,768]{1,0:T(8,128)(2,1)} %bitcast.18, ...), custom_call_target="tpu_custom_call" | custom-call | tf_op jit(solution)/shard_map/layer/pallas_call | solution.py:975
  154.2 0.0 copy-start
  154.2 1.4 slice_reduce_fusion
  155.6 0.7 slice.30
  156.3 1.5 fusion
  157.8 0.7 reshape.59
  158.5 2.0 %copy.41 = bf16[768,480]{0,1:T(8,128)(2,1)} copy(bf16[768,480]{0,1:T(8,128)(2,1)} %bitcast.19) | data formatting | bytes 1474560
  160.5 0.0 copy-done
  160.5 0.0 copy-start.1
  160.5 1.1 copy.42
  161.6 0.5 copy-done.1
  162.1 0.0 copy-start.2
  162.1 0.0 copy-start.4
  162.1 0.0 copy-start.3
  162.1 0.9 copy.43
  163.0 0.3 copy-done.2
  163.3 0.7 copy.44
  164.0 0.0 copy-done.4
  164.0 0.6 copy.45
  164.7 0.0 copy-done.3
  164.7 0.6 copy.46
Async XLA Ops:
  154.2 6.3 %copy-start = (f32[480,768]{1,0:T(8,128)S(1)}, f32[480,768]{1,0:T(8,128)}, u32[]{:S(2)}) copy-start(f32[480,768]{1,0:T(8,128)} %get-tuple-element.22) | copy-start | bytes 4423684
  160.5 1.6 copy-start.1
  162.1 1.2 copy-start.2
  162.1 1.9 %copy-start.4 = (f32[120,240]{1,0:T(8,128)S(1)}, f32[120,240]{1,0:T(8,128)}, u32[]{:S(2)}) copy-start(f32[120,240]{1,0:T(8,128)} %get-tuple-element.58) | copy-start | bytes 345604
  162.1 2.5 %copy-start.3 = (f32[240,120]{1,0:T(8,128)S(1)}, f32[240,120]{1,0:T(8,128)}, u32[]{:S(2)}) copy-start(f32[240,120]{1,0:T(8,128)} %get-tuple-element.60) | copy-start | bytes 345604
